TPU v7x, 32 devices: a whole 2x2x4 slice. The times are simulated.
32 devices in a mesh: date: 2 (over core), space: 16 (over z, y, x).
Axes of the slice: x: 2, y: 2, z: 4, core: 2. Of those that a mesh axis runs over, the one named last changes fastest.
Arguments:
- acquisitions: bfloat16 [16, 2048, 512], P('date', 'space')
- partner: int32 [16, 9], replicated, may hold values from 0 to 15, as said below
- pair_count: int32 [16], replicated, may hold values from 2 to 9, as said below
- band_low: int32 [16, 9], P('date'), may hold values from 0 to 95
- band_high: int32 [16, 9], P('date'), may hold values from 160 to 256
Outputs:
- coherence: bfloat16 [16, 9, 2048, 512], P('date', None, 'space')
Inputs may be any that keep to these rules, and one draw needn't show every extreme that they name: For j < pair_count[d], partner[d, j] is the secondary date of pair j of date d; other slots name any date but no pair. A secondary never lies in its reference's block of 8 dates (one index of date), and the pairs of one block name at most 4 distinct dates of any other block; some two blocks reach 4. The pairs of date d are its first pair_count[d] slots.
All inputs are finite; a program needn't handle non-finite values.
Results may differ from a plain program's by a relative error of at most 0.0085.
Values may be sent and summed in bfloat16 or wider, within the bound.
No kernel may reach another device: no remote copies, remote signals or barrier semaphores. Data moves between devices by JAX's collectives and lax.ppermute only.
A program may use at most 192 MiB of HBM per device.

v0:
```python
import functools

import jax
import jax.numpy as jnp
import ml_dtypes
import numpy as np
from jax import lax
from jax.experimental import pallas as pl
from jax.experimental.pallas import tpu as pltpu
from jax.sharding import PartitionSpec as P

BF = jnp.bfloat16
F32 = jnp.float32
LANES = 16
GROUP = 3


def constants(bins, rows):
    k = np.arange(bins)
    angle = (k[:, None] * k[None, :] % bins) * (2.0 * np.pi / bins)
    cosine, sine = np.cos(angle), np.sin(angle)
    forward = np.block([[cosine, -sine], [sine, cosine]])
    inverse = np.block([[cosine, sine], [-sine, cosine]]) / bins
    half = bins // 2
    even, odd = np.arange(0, bins, 2), np.arange(1, bins, 2)
    even, odd = np.concatenate([even, bins + even]), np.concatenate([odd, bins + odd])
    first = np.concatenate([np.arange(half), bins + np.arange(half)])
    band = np.abs(k[:, None] - k[None, :]) <= 4
    tiles = rows // LANES
    order = np.zeros(((tiles + 2) * LANES, rows))
    for g in range(-1, tiles + 1):
        for s in range(LANES):
            row = s * tiles + g
            if 0 <= row < rows:
                order[(g + 1) * LANES + s, row] = 1
    made = (forward[:, np.concatenate([even, odd])], inverse[even][:, first], inverse[odd][:, first], band, order)
    return [jnp.asarray(m.astype(np.float32).astype(ml_dtypes.bfloat16)) for m in made]


def dot(a, b):
    return lax.dot_general(a, b, (((1,), (0,)), ((), ())), preferred_element_type=F32)


def pairs_kernel(
    block, count, partner, low, high, *refs, blocks
):
    strips, refs = refs[:blocks], refs[blocks:]
    edges, refs = refs[:blocks], refs[blocks:]
    forward, inv_even, inv_odd, band, order, out, spectra, turned = refs
    date = pl.program_id(0)
    dates, rows, cols = strips[0].shape
    slots = out.shape[1]
    ext = spectra.shape[1]
    bins = cols // 2
    half = bins // 2

    @pl.when(date == 0)
    def _():
        table, place = forward[...], order[...]
        row_id = lax.broadcasted_iota(jnp.int32, (ext, 2 * dates), 0)
        col_id = lax.broadcasted_iota(jnp.int32, (ext, 2 * dates), 1)
        for k in range(blocks):
            edge = dot(edges[k][...], table).astype(BF)
            for q in range(dates):
                at_edge = ((row_id == 0) & (col_id == q)) | ((row_id == ext - 1) & (col_id == dates + q))
                spectrum = dot(strips[k][q], table).astype(BF)
                put = jnp.where(at_edge, 1.0, 0.0).astype(BF)
                spectra[k * dates + q] = (dot(place, spectrum) + dot(put, edge)).astype(BF)

    lane = lax.broadcasted_iota(jnp.int32, (LANES, cols), 1)
    bin_id = lane % half * 2 + lane // bins
    here = block[0]
    whole_date = here * dates + date
    even, odd, window = inv_even[...], inv_odd[...], band[...]

    def masked(slot):
        live = slot < count[whole_date]
        low_bin = jnp.where(live, low[date, slot], 0)
        high_bin = jnp.where(live, high[date, slot], 0)
        mask = jnp.where((bin_id >= low_bin) & (bin_id < high_bin), 1.0, 0.0).astype(BF)[None]
        second = partner[whole_date, slot]
        away = second // dates - here
        away = jnp.where(away < 0, away + blocks, away)
        tiled = (ext // LANES, LANES, cols)
        a = (spectra[date].reshape(tiled) * mask).reshape(ext, cols)
        b = (spectra[away * dates + second % dates].reshape(tiled) * mask).reshape(ext, cols)
        return [a, b]

    def some_slots(step, _):
        group = [step * GROUP + i for i in range(GROUP)]
        x = jnp.concatenate([m for slot in group for m in masked(slot)], 0)
        e = dot(x[:, :bins], even)
        o = dot(x[:, bins:], odd)
        halves = ((e + o).astype(BF), (e - o).astype(BF))
        sums = []
        for i in range(GROUP):
            fields = []
            for v in halves:
                a, b = v[2 * i * ext : (2 * i + 1) * ext], v[(2 * i + 1) * ext : (2 * i + 2) * ext]
                a_re, a_im, b_re, b_im = a[:, :half], a[:, half:], b[:, :half], b[:, half:]
                fields.append(
                    [
                        a_re * b_re + a_im * b_im,
                        a_im * b_re - a_re * b_im,
                        a_re * a_re + a_im * a_im,
                        b_re * b_re + b_im * b_im,
                    ]
                )
            for first, second in zip(*fields):
                f = jnp.concatenate([first, second], 1)
                sums.append(f[:rows] + f[LANES : LANES + rows] + f[2 * LANES :])
        looked = dot(jnp.concatenate(sums, 0), window)
        for i, slot in enumerate(group):
            cross_re, cross_im, power_ref, power_sec = [
                looked[(4 * i + q) * rows : (4 * i + q + 1) * rows] for q in range(4)
            ]
            scale = lax.rsqrt(jnp.maximum(power_ref, 1.0) * jnp.maximum(power_sec, 1.0))
            re, im = cross_re * scale, cross_im * scale
            tiles = rows // LANES
            for c, v in enumerate((re[:, :half], re[:, half:], im[:, :half], im[:, half:])):
                for g in range(tiles):
                    turned[i, c, pl.ds(g, LANES, stride=tiles), :] = v[g * LANES : (g + 1) * LANES]
            out[0, slot] = jnp.concatenate([turned[i, c] for c in range(4)], 1).astype(BF)
        return 0

    lax.fori_loop(0, slots // GROUP, some_slots, 0)


def pairs(block, count, partner, low, high, strips, edges):
    dates, rows, cols = strips[0].shape
    slots = partner.shape[1]
    tables = constants(cols // 2, rows)
    scalars = pl.BlockSpec(memory_space=pltpu.SMEM)
    whole = pl.BlockSpec(memory_space=pltpu.VMEM)
    blocks = len(strips)
    return pl.pallas_call(
        functools.partial(pairs_kernel, blocks=blocks),
        grid=(dates,),
        in_specs=[scalars] * 5 + [whole] * (2 * blocks + len(tables)),
        out_specs=pl.BlockSpec((1, slots, rows, cols), lambda d: (d, 0, 0, 0)),
        out_shape=jax.ShapeDtypeStruct((dates, slots, rows, cols), BF),
        scratch_shapes=[
            pltpu.VMEM((blocks * dates, rows + 2 * LANES, cols), BF),
            pltpu.VMEM((GROUP, 4, rows, cols // 4), F32),
        ],
        compiler_params=pltpu.CompilerParams(vmem_limit_bytes=48 * 2**20),
    )(block, count, partner, low, high, *strips, *edges, *tables)


def local(acquisitions, partner, pair_count, band_low, band_high):
    blocks = lax.axis_size("date")
    strips_count = lax.axis_size("space")
    up = [(i, i + 1) for i in range(strips_count - 1)]
    down = [(i + 1, i) for i in range(strips_count - 1)]
    before = lax.ppermute(acquisitions[:, -1, :], "space", up)
    after = lax.ppermute(acquisitions[:, 0, :], "space", down)
    edge = jnp.concatenate([before, after], 0)

    def from_ahead(x, k):
        return lax.ppermute(x, "date", [((i + k) % blocks, i) for i in range(blocks)]) if k else x

    strips = [from_ahead(acquisitions, k) for k in range(blocks)]
    edges = [from_ahead(edge, k) for k in range(blocks)]
    block = lax.axis_index("date").reshape(1).astype(jnp.int32)
    return pairs(block, pair_count, partner, band_low, band_high, strips, edges)


def solution(mesh):
    placed = (P("date", "space", None), P(), P(), P("date", None), P("date", None))
    return jax.shard_map(
        local, mesh=mesh, in_specs=placed, out_specs=P("date", None, "space", None), check_vma=False
    )
```

profile of v0, /device:TPU:15, one launch (start us, length us, event | category | flops | bytes accessed | tf_op | source)
XLA Modules:
  0.0 54.0 jit_solution(14158606037044329)
XLA Ops:
  0.0 0.7 %collective-permute-start = (bf16[8,128,512]{2,1,0:T(8,128)(2,1)}, bf16[8,128,512]{2,1,0:T(8,128)(2,1)S(1)}, u32[]{:S(2)}, u32[]{:S(2)}) collective-permute-start(bf16[8,128,512]{2,1,0:T(8,128)(2,1)} %refs_0_.1), channel_id=1, source_target_pairs={{16,0},{0,16},{17,1},{1,17},{18,2},{2,18},{19,3},{3,19},{20,4},{4,... | collective-permute-start | bytes 3145736 | tf_op jit(solution)/shard_map/ppermute | solution.py:160
  0.7 0.9 %fusion = (bf16[8,1,512]{2,1,0:T(2,128)(2,1)S(1)}, bf16[8,1,512]{2,1,0:T(2,128)(2,1)S(1)}) fusion(bf16[8,128,512]{2,1,0:T(8,128)(2,1)} %refs_0_.1), kind=kLoop, calls=%fused_computation.4 | loop fusion | bytes 32768 | tf_op jit(solution)/shard_map/slice | solution.py:156
  1.6 3.1 %collective-permute-start.1 = (bf16[8,512]{1,0:T(8,128)(2,1)S(1)}, bf16[8,512]{1,0:T(8,128)(2,1)S(1)}, u32[]{:S(2)}, u32[]{:S(2)}) collective-permute-start(bf16[8,512]{1,0:T(8,128)(2,1)S(1)} %bitcast.7), channel_id=1, source_target_pairs={{0,1},{1,2},{2,3},{3,4},{4,5},{5,6},{6,7},{7,8},{8,9},{9,10},{10,1... | collective-permute-start | bytes 24584 | tf_op jit(solution)/shard_map/ppermute | solution.py:155
  4.7 2.2 %collective-permute-start.2 = (bf16[8,512]{1,0:T(8,128)(2,1)S(1)}, bf16[8,512]{1,0:T(8,128)(2,1)S(1)}, u32[]{:S(2)}, u32[]{:S(2)}) collective-permute-start(bf16[8,512]{1,0:T(8,128)(2,1)S(1)} %bitcast.8), channel_id=1, source_target_pairs={{1,0},{2,1},{3,2},{4,3},{5,4},{6,5},{7,6},{8,7},{9,8},{10,9},{11,1... | collective-permute-start | bytes 24584 | tf_op jit(solution)/shard_map/ppermute | solution.py:156
  6.9 0.0 collective-permute-done.1
  6.9 4.0 %collective-permute-done.2 = bf16[8,512]{1,0:T(8,128)(2,1)S(1)} collective-permute-done((bf16[8,512]{1,0:T(8,128)(2,1)S(1)}, bf16[8,512]{1,0:T(8,128)(2,1)S(1)}, u32[]{:S(2)}, u32[]{:S(2)}) %collective-permute-start.2) | collective-permute-done | bytes 8224 | tf_op jit(solution)/shard_map/ppermute | solution.py:156
  10.9 1.4 %collective-permute-start.3 = (bf16[16,512]{1,0:T(8,128)(2,1)S(1)}, bf16[16,512]{1,0:T(8,128)(2,1)S(1)}, u32[]{:S(2)}, u32[]{:S(2)}) collective-permute-start(bf16[16,512]{1,0:T(8,128)(2,1)S(1)} %constant_dynamic-update-slice_fusion.refs_2_), channel_id=1, source_target_pairs={{16,0},{0,16},{17,1},{1,17},{18,2},{2,18},{19,3},{3,19},{20,4},{4,... | collective-permute-start | bytes 49160 | tf_op jit(solution)/shard_map/ppermute | solution.py:160
  12.4 0.8 %collective-permute-done.3.refs_3_ = bf16[16,512]{1,0:T(8,128)(2,1)S(1)} collective-permute-done((bf16[16,512]{1,0:T(8,128)(2,1)S(1)}, bf16[16,512]{1,0:T(8,128)(2,1)S(1)}, u32[]{:S(2)}, u32[]{:S(2)}) %collective-permute-start.3) | collective-permute-done | bytes 16416 | tf_op jit(solution)/shard_map/ppermute | solution.py:160
  13.2 0.0 collective-permute-done.refs_1_
  13.2 0.0 copy-start
  13.2 1.2 %copy-done = bf16[8,128,512]{2,1,0:T(8,128)(2,1)S(1)} copy-done((bf16[8,128,512]{2,1,0:T(8,128)(2,1)S(1)}, bf16[8,128,512]{2,1,0:T(8,128)(2,1)}, u32[]{:S(2)}) %copy-start) | copy-done | bytes 1048600
  14.4 0.0 copy-start.1
  14.4 1.0 %copy-done.1 = bf16[512,512]{1,0:T(8,128)(2,1)S(1)} copy-done((bf16[512,512]{1,0:T(8,128)(2,1)S(1)}, bf16[512,512]{1,0:T(8,128)(2,1)}, u32[]{:S(2)}) %copy-start.1) | copy-done | bytes 524312
  15.5 0.0 copy-start.2
  15.5 0.9 %copy-done.2 = bf16[256,256]{1,0:T(8,128)(2,1)S(1)} copy-done((bf16[256,256]{1,0:T(8,128)(2,1)S(1)}, bf16[256,256]{1,0:T(8,128)(2,1)}, u32[]{:S(2)}) %copy-start.2) | copy-done | bytes 131096
  16.4 0.0 copy-start.3
  16.4 0.9 %copy-done.3 = bf16[256,256]{1,0:T(8,128)(2,1)S(1)} copy-done((bf16[256,256]{1,0:T(8,128)(2,1)S(1)}, bf16[256,256]{1,0:T(8,128)(2,1)}, u32[]{:S(2)}) %copy-start.3) | copy-done | bytes 131096
  17.3 0.9 %copy-done.4 = bf16[256,256]{1,0:T(8,128)(2,1)S(1)} copy-done((bf16[256,256]{1,0:T(8,128)(2,1)S(1)}, bf16[256,256]{1,0:T(8,128)(2,1)}, u32[]{:S(2)}) %copy-start.4) | copy-done | bytes 131096
  18.2 0.8 %copy-done.5 = bf16[160,128]{1,0:T(8,128)(2,1)S(1)} copy-done((bf16[160,128]{1,0:T(8,128)(2,1)S(1)}, bf16[160,128]{1,0:T(8,128)(2,1)}, u32[]{:S(2)}) %copy-start.5) | copy-done | bytes 40984
  19.0 0.7 %copy-done.6 = s32[16,9]{1,0:T(8,128)S(1)} copy-done((s32[16,9]{1,0:T(8,128)S(1)}, s32[16,9]{1,0:T(8,128)}, u32[]{:S(2)}) %copy-start.6) | copy-done | bytes 600
  19.7 0.7 %copy-done.7 = s32[8,9]{1,0:T(8,128)S(1)} copy-done((s32[8,9]{1,0:T(8,128)S(1)}, s32[8,9]{1,0:T(8,128)}, u32[]{:S(2)}) %copy-start.7) | copy-done | bytes 312
  20.4 0.7 %copy-done.8 = s32[8,9]{1,0:T(8,128)S(1)} copy-done((s32[8,9]{1,0:T(8,128)S(1)}, s32[8,9]{1,0:T(8,128)}, u32[]{:S(2)}) %copy-start.8) | copy-done | bytes 312
  21.0 0.7 %copy-done.9 = s32[16]{0:T(128)S(1)} copy-done((s32[16]{0:T(128)S(1)}, s32[16]{0:T(128)}, u32[]{:S(2)}) %copy-start.9) | copy-done | bytes 88
  21.7 32.3 %shard_map.100 = bf16[8,9,128,512]{3,2,1,0:T(8,128)(2,1)} custom-call(s32[1]{0:T(128)} %bitcast.block, s32[16]{0:T(128)S(1)} %copy-done.9, s32[16,9]{1,0:T(8,128)S(1)} %copy-done.6, s32[8,9]{1,0:T(8,128)S(1)} %copy-done.7, s32[8,9]{1,0:T(8,128)S(1)} %copy-done.8, bf16[8,128,512]{2,1,0:T(8,128)(2,1)S(1)} %copy-done, ...), custom_call_target="tpu_custom_call" | custom-call | tf_op jit(solution)/shard_map/pallas_call | solution.py:136
  (10 shorter events, 0.0 us)
Async XLA Ops:
  0.0 13.2 %collective-permute-start = (bf16[8,128,512]{2,1,0:T(8,128)(2,1)}, bf16[8,128,512]{2,1,0:T(8,128)(2,1)S(1)}, u32[]{:S(2)}, u32[]{:S(2)}) collective-permute-start(bf16[8,128,512]{2,1,0:T(8,128)(2,1)} %refs_0_.1), channel_id=1, source_target_pairs={{16,0},{0,16},{17,1},{1,17},{18,2},{2,18},{19,3},{3,19},{20,4},{4,... | collective-permute-start | bytes 3145736 | tf_op jit(solution)/shard_map/ppermute | solution.py:160
  1.6 5.3 %collective-permute-start.1 = (bf16[8,512]{1,0:T(8,128)(2,1)S(1)}, bf16[8,512]{1,0:T(8,128)(2,1)S(1)}, u32[]{:S(2)}, u32[]{:S(2)}) collective-permute-start(bf16[8,512]{1,0:T(8,128)(2,1)S(1)} %bitcast.7), channel_id=1, source_target_pairs={{0,1},{1,2},{2,3},{3,4},{4,5},{5,6},{6,7},{7,8},{8,9},{9,10},{10,1... | collective-permute-start | bytes 24584 | tf_op jit(solution)/shard_map/ppermute | solution.py:155
  4.7 6.2 %collective-permute-start.2 = (bf16[8,512]{1,0:T(8,128)(2,1)S(1)}, bf16[8,512]{1,0:T(8,128)(2,1)S(1)}, u32[]{:S(2)}, u32[]{:S(2)}) collective-permute-start(bf16[8,512]{1,0:T(8,128)(2,1)S(1)} %bitcast.8), channel_id=1, source_target_pairs={{1,0},{2,1},{3,2},{4,3},{5,4},{6,5},{7,6},{8,7},{9,8},{10,9},{11,1... | collective-permute-start | bytes 24584 | tf_op jit(solution)/shard_map/ppermute | solution.py:156
  10.9 2.3 %collective-permute-start.3 = (bf16[16,512]{1,0:T(8,128)(2,1)S(1)}, bf16[16,512]{1,0:T(8,128)(2,1)S(1)}, u32[]{:S(2)}, u32[]{:S(2)}) collective-permute-start(bf16[16,512]{1,0:T(8,128)(2,1)S(1)} %constant_dynamic-update-slice_fusion.refs_2_), channel_id=1, source_target_pairs={{16,0},{0,16},{17,1},{1,17},{18,2},{2,18},{19,3},{3,19},{20,4},{4,... | collective-permute-start | bytes 49160 | tf_op jit(solution)/shard_map/ppermute | solution.py:160
  13.2 1.2 %copy-start = (bf16[8,128,512]{2,1,0:T(8,128)(2,1)S(1)}, bf16[8,128,512]{2,1,0:T(8,128)(2,1)}, u32[]{:S(2)}) copy-start(bf16[8,128,512]{2,1,0:T(8,128)(2,1)} %refs_0_.1) | copy-start | bytes 3145732
  14.4 1.0 %copy-start.1 = (bf16[512,512]{1,0:T(8,128)(2,1)S(1)}, bf16[512,512]{1,0:T(8,128)(2,1)}, u32[]{:S(2)}) copy-start(bf16[512,512]{1,0:T(8,128)(2,1)} %constant.16.clone.refs_4_) | copy-start | bytes 1572868
  15.5 0.9 %copy-start.2 = (bf16[256,256]{1,0:T(8,128)(2,1)S(1)}, bf16[256,256]{1,0:T(8,128)(2,1)}, u32[]{:S(2)}) copy-start(bf16[256,256]{1,0:T(8,128)(2,1)} %constant.19.clone.refs_7_) | copy-start | bytes 393220
  16.4 0.9 %copy-start.3 = (bf16[256,256]{1,0:T(8,128)(2,1)S(1)}, bf16[256,256]{1,0:T(8,128)(2,1)}, u32[]{:S(2)}) copy-start(bf16[256,256]{1,0:T(8,128)(2,1)} %constant.18.clone.refs_6_) | copy-start | bytes 393220
  17.3 0.9 %copy-start.4 = (bf16[256,256]{1,0:T(8,128)(2,1)S(1)}, bf16[256,256]{1,0:T(8,128)(2,1)}, u32[]{:S(2)}) copy-start(bf16[256,256]{1,0:T(8,128)(2,1)} %constant.17.clone.refs_5_) | copy-start | bytes 393220
  18.2 0.8 %copy-start.5 = (bf16[160,128]{1,0:T(8,128)(2,1)S(1)}, bf16[160,128]{1,0:T(8,128)(2,1)}, u32[]{:S(2)}) copy-start(bf16[160,128]{1,0:T(8,128)(2,1)} %constant.20.clone.refs_8_) | copy-start | bytes 122884
  19.0 0.7 %copy-start.6 = (s32[16,9]{1,0:T(8,128)S(1)}, s32[16,9]{1,0:T(8,128)}, u32[]{:S(2)}) copy-start(s32[16,9]{1,0:T(8,128)} %partner.1) | copy-start | bytes 1732
  19.7 0.7 %copy-start.7 = (s32[8,9]{1,0:T(8,128)S(1)}, s32[8,9]{1,0:T(8,128)}, u32[]{:S(2)}) copy-start(s32[8,9]{1,0:T(8,128)} %low.1) | copy-start | bytes 868
  20.4 0.7 %copy-start.8 = (s32[8,9]{1,0:T(8,128)S(1)}, s32[8,9]{1,0:T(8,128)}, u32[]{:S(2)}) copy-start(s32[8,9]{1,0:T(8,128)} %high.1) | copy-start | bytes 868
  21.0 0.7 %copy-start.9 = (s32[16]{0:T(128)S(1)}, s32[16]{0:T(128)}, u32[]{:S(2)}) copy-start(s32[16]{0:T(128)} %count.1) | copy-start | bytes 196
where the time goes:
time: 54.5 us; the launch traced here: 54 us
  Pallas kernels  32.3 us (59%)
  local copies, waits for them, and re-layouts  9.39 us (17%)
  starting transfers between devices  7.39 us (14%)
  waiting for transfers between devices  4.85 us (9%)
    pallas_call x1, Pallas kernels, pairs(): pl.pallas_call(functools.partial(pairs_kernel, blocks=blocks), grid=(date...  32.3 us
    unnamed x23, local copies, waits for them, and re-layouts  8.49 us
    ppermute x1, waiting for transfers between devices, local(): after = lax.ppermute(acquisitions[:, 0, :], 'space', down)  4 us
    ppermute x1, starting transfers between devices, local(): before = lax.ppermute(acquisitions[:, -1, :], 'space', up)  3.12 us
    ppermute x1, starting transfers between devices, local(): after = lax.ppermute(acquisitions[:, 0, :], 'space', down)  2.16 us
    ppermute x2, starting transfers between devices, from_ahead(): lax.ppermute(x, 'date', [((i + k) % blocks, i) for i in range(blocks)])  2.11 us
  transfers between devices with their start and end apart: 4, of which 2 were waited for; matrix products, arithmetic and copies ran while one was open for 2% of the time, Pallas kernels for 0%

commit v1 on v0

v1 whole, which is shorter than its diff:
```python
import functools

import jax
import jax.numpy as jnp
import ml_dtypes
import numpy as np
from jax import lax
from jax.experimental import pallas as pl
from jax.experimental.pallas import tpu as pltpu
from jax.sharding import PartitionSpec as P

BF = jnp.bfloat16
F32 = jnp.float32
TILE = 16
SUB = 8


def constants(bins):
    k = np.arange(bins)
    angle = (k[:, None] * k[None, :] % bins) * (2.0 * np.pi / bins)
    cosine, sine = np.cos(angle), np.sin(angle)
    forward = np.block([[cosine, -sine], [sine, cosine]])
    inverse = np.block([[cosine, sine], [-sine, cosine]]) / bins
    half = bins // 2
    even, odd = np.arange(0, bins, 2), np.arange(1, bins, 2)
    even, odd = np.concatenate([even, bins + even]), np.concatenate([odd, bins + odd])
    first = np.concatenate([np.arange(half), bins + np.arange(half)])
    band = np.abs(k[:, None] - k[None, :]) <= 4
    made = (forward[:, np.concatenate([even, odd])], inverse[even][:, first], inverse[odd][:, first], band)
    return [jnp.asarray(m.astype(np.float32).astype(ml_dtypes.bfloat16)) for m in made]


def dot(a, b):
    return lax.dot_general(a, b, (((1,), (0,)), ((), ())), preferred_element_type=F32)


def pairs_kernel(block, count, partner, low, high, *refs, blocks):
    mains, edges, refs = refs[:blocks], refs[blocks : 2 * blocks], refs[2 * blocks :]
    forward, inv_even, inv_odd, band, out = refs[:5]
    spectra, sums, across, ready, main_sem, out_sem = refs[5:]
    dates, slots = low.shape
    ext, cols = spectra.shape[1:]
    rows = ext - TILE
    bins = cols // 2
    half = bins // 2
    here = block[0]

    def main_copy(k):
        place = spectra.at[pl.ds(k * dates, dates), pl.ds(0, rows)]
        return pltpu.make_async_copy(mains[k], place, main_sem.at[k])

    for k in range(blocks):
        main_copy(k).start()

    tile_row = lax.broadcasted_iota(jnp.int32, (TILE, cols), 0)
    for k in range(blocks):
        edge = dot(edges[k][...], forward[...]).astype(BF).astype(F32)
        for q in range(dates):
            before, after = edge[q : q + 1], edge[dates + q : dates + q + 1]
            tile = jnp.where(tile_row == 0, after, jnp.where(tile_row == TILE - 1, before, 0.0))
            spectra[k * dates + q, rows:ext] = tile.astype(BF)

    lane = lax.broadcasted_iota(jnp.int32, (TILE, cols), 1)
    bin_id = lane % half * 2 + lane // bins
    even, odd, window = inv_even[...], inv_odd[...], band[...]

    def masked(date, slot):
        whole_date = here * dates + date
        live = slot < count[whole_date]
        low_bin = jnp.where(live, low[date, slot], 0)
        high_bin = jnp.where(live, high[date, slot], 0)
        mask = jnp.where((bin_id >= low_bin) & (bin_id < high_bin), 1.0, 0.0).astype(BF)[None]
        second = partner[whole_date, slot]
        away = second // dates - here
        away = jnp.where(away < 0, away + blocks, away)
        tiled = (ext // TILE, TILE, cols)
        a = (spectra[date].reshape(tiled) * mask).reshape(ext, cols)
        b = (spectra[away * dates + second % dates].reshape(tiled) * mask).reshape(ext, cols)
        return [a, b]

    def filter_date(date, ring):
        x = jnp.concatenate([m for slot in range(slots) for m in masked(date, slot)], 0)
        e = dot(x[:, :bins], even)
        o = dot(x[:, bins:], odd)
        for slot in range(slots):
            r = slice(2 * slot * ext, (2 * slot + 2) * ext)
            for c, v in enumerate(((e[r] + o[r]).astype(BF), (e[r] - o[r]).astype(BF))):
                a_re, a_im, b_re, b_im = v[:ext, :half], v[:ext, half:], v[ext:, :half], v[ext:, half:]
                fields = (
                    a_re * b_re + a_im * b_im,
                    a_im * b_re - a_re * b_im,
                    a_re * a_re + a_im * a_im,
                    b_re * b_re + b_im * b_im,
                )
                for q, field in enumerate(fields):
                    sums[ring, slot, q * ext : (q + 1) * ext, c * half : (c + 1) * half] = field

    def look_date(ring):
        cut = slots // 2
        groups = [list(range(cut)), list(range(cut, slots))]
        summed = []
        for group in groups:
            if group:
                y = dot(jnp.concatenate([sums[ring, slot] for slot in group], 0), window)
                summed += [y[4 * i * ext : 4 * (i + 1) * ext] for i in range(len(group))]
        for slot in range(slots):
            looked = []
            for q in range(4):
                parts = []
                for c in range(2):
                    v = summed[slot][q * ext : (q + 1) * ext, c * half : (c + 1) * half]
                    held = across.at[slot, 2 * q + c]
                    held[0:SUB] = v[ext - SUB :]
                    held[SUB:ext] = v[: ext - SUB]
                    parts.append(
                        held[SUB - 1 : SUB - 1 + rows] + held[SUB : SUB + rows] + held[SUB + 1 : SUB + 1 + rows]
                    )
                looked.append(jnp.concatenate(parts, 1))
            scale = lax.rsqrt(jnp.maximum(looked[2], 1.0) * jnp.maximum(looked[3], 1.0))
            ready[ring, slot, :, :bins] = (looked[0] * scale).astype(BF)
            ready[ring, slot, :, bins:] = (looked[1] * scale).astype(BF)

    def send(date, ring):
        return pltpu.make_async_copy(ready.at[ring], out.at[date], out_sem.at[ring])

    for k in range(blocks):
        main_copy(k).wait()
    filter_date(0, 0)

    def body(date, _):
        now = lax.rem(date, 2)
        last = 1 - now

        @pl.when(date >= 3)
        def _():
            send(date - 3, last).wait()

        look_date(last)
        filter_date(date, now)
        send(date - 1, last).start()
        return 0

    lax.fori_loop(1, dates, body, 0)
    end = (dates - 1) % 2
    if dates >= 3:
        send(dates - 3, end).wait()
    look_date(end)
    send(dates - 1, end).start()
    if dates >= 2:
        send(dates - 2, 1 - end).wait()
    send(dates - 1, end).wait()


def pairs(block, count, partner, low, high, mains, edges, tables):
    dates, rows, cols = mains[0].shape
    slots = partner.shape[1]
    ext = rows + TILE
    scalars = pl.BlockSpec(memory_space=pltpu.SMEM)
    whole = pl.BlockSpec(memory_space=pltpu.VMEM)
    anywhere = pl.BlockSpec(memory_space=pl.ANY)
    blocks = len(mains)
    work = dates * slots * rows * cols
    return pl.pallas_call(
        functools.partial(pairs_kernel, blocks=blocks),
        in_specs=[scalars] * 5 + [anywhere] * blocks + [whole] * (blocks + len(tables)),
        out_specs=anywhere,
        out_shape=jax.ShapeDtypeStruct((dates, slots, rows, cols), BF),
        scratch_shapes=[
            pltpu.VMEM((blocks * dates, ext, cols), BF),
            pltpu.VMEM((2, slots, 4 * ext, cols // 2), BF),
            pltpu.VMEM((slots, 8, ext, cols // 4), F32),
            pltpu.VMEM((2, slots, rows, cols), BF),
            pltpu.SemaphoreType.DMA((blocks,)),
            pltpu.SemaphoreType.DMA((2,)),
        ],
        cost_estimate=pl.CostEstimate(flops=work * cols * 4, bytes_accessed=work * 2, transcendentals=work // 2),
        compiler_params=pltpu.CompilerParams(vmem_limit_bytes=58 * 2**20),
    )(block, count, partner, low, high, *mains, *edges, *tables)


def edge_rows(strips):
    n = lax.axis_size("space")
    even = lax.axis_index("space") % 2 == 0
    first, last = strips[:, 0, :], strips[:, -1, :]
    inner = [(i, i ^ 1) for i in range(n) if i ^ 1 < n]
    outer = [(i, i + 1) for i in range(1, n - 1, 2)] + [(i + 1, i) for i in range(1, n - 1, 2)]
    from_inner = lax.ppermute(jnp.where(even, last, first), "space", inner)
    from_outer = lax.ppermute(jnp.where(even, first, last), "space", outer)
    return jnp.concatenate([jnp.where(even, from_outer, from_inner), jnp.where(even, from_inner, from_outer)], 0)


def local(acquisitions, partner, pair_count, band_low, band_high):
    blocks = lax.axis_size("date")
    dates, rows, cols = acquisitions.shape
    tables = constants(cols // 2)

    def from_ahead(x, k):
        return lax.ppermute(x, "date", [((i + k) % blocks, i) for i in range(blocks)]) if k else x

    edge = edge_rows(acquisitions)
    mains = []
    for k in range(blocks):
        strip = from_ahead(acquisitions, k).reshape(dates * rows, cols)
        spectrum = jnp.dot(strip, tables[0], preferred_element_type=F32).astype(BF)
        mains.append(spectrum.reshape(dates, rows, cols))
    edges = [from_ahead(edge, k) for k in range(blocks)]
    block = lax.axis_index("date").reshape(1).astype(jnp.int32)
    return pairs(block, pair_count, partner, band_low, band_high, mains, edges, tables)


def solution(mesh):
    placed = (P("date", "space", None), P(), P(), P("date", None), P("date", None))
    return jax.shard_map(
        local, mesh=mesh, in_specs=placed, out_specs=P("date", None, "space", None), check_vma=False
    )
```

time: 54.5 us -> 35.2 us (0.65)
  the two profiles are of different devices: /device:TPU:15 before, /device:TPU:0 now
where the time goes in v1:
time: 35.2 us; the launch traced here: 34.9 us
  Pallas kernels  21.2 us (60%)
  starting transfers between devices  6.48 us (18%)
  local copies, waits for them, and re-layouts  4.15 us (12%)
  matrix products  2.96 us (8%)
    pallas_call x1, Pallas kernels, pairs(): pl.pallas_call(functools.partial(pairs_kernel, blocks=blocks), in_specs=[...  21.2 us
    ppermute x1, starting transfers between devices, edge_rows(): from_inner = lax.ppermute(jnp.where(even, last, first), 'space', inner)  5.29 us
    dot_general x2, matrix products, local(): spectrum = jnp.dot(strip, tables[0], preferred_element_type=F32).astype(BF)  2.96 us
    convert_element_type x2, local copies, waits for them, and re-layouts, local(): spectrum = jnp.dot(strip, tables[0], preferred_element_type=F32).astype(BF)  2.64 us
    slice x1, local copies, waits for them, and re-layouts, edge_rows(): first, last = (strips[:, 0, :], strips[:, -1, :])  0.9 us
  transfers between devices with their start and end apart: 4, of which 0 were waited for; matrix products, arithmetic and copies ran while one was open for 19% of the time, Pallas kernels for 0%

profile of v1, /device:TPU:0, one launch (start us, length us, event | category | flops | bytes accessed | tf_op | source)
XLA Modules:
  0.0 34.9 jit_solution(13920081243614672676)
XLA Ops:
  0.0 0.5 %collective-permute-start = (bf16[8,128,512]{2,1,0:T(8,128)(2,1)}, bf16[8,128,512]{2,1,0:T(8,128)(2,1)S(1)}, u32[]{:S(2)}, u32[]{:S(2)}) collective-permute-start(bf16[8,128,512]{2,1,0:T(8,128)(2,1)} %param.9), channel_id=1, source_target_pairs={{16,0},{0,16},{17,1},{1,17},{18,2},{2,18},{19,3},{3,19},{20,4},{4,... | collective-permute-start | bytes 3145736 | tf_op jit(solution)/shard_map/ppermute | solution.py:198
  0.5 0.9 %fusion.2 = (bf16[8,1,512]{2,1,0:T(2,128)(2,1)S(1)}, bf16[8,1,512]{2,1,0:T(2,128)(2,1)S(1)}) fusion(bf16[8,128,512]{2,1,0:T(8,128)(2,1)} %param.9), kind=kLoop, calls=%fused_computation.9 | loop fusion | bytes 32768 | tf_op jit(solution)/shard_map/slice | solution.py:184
  1.4 0.7 %collective-permute-start.1 = (bf16[8,512]{1,0:T(8,128)(2,1)S(1)}, bf16[8,512]{1,0:T(8,128)(2,1)S(1)}, u32[]{:S(2)}, u32[]{:S(2)}) collective-permute-start(bf16[8,512]{1,0:T(8,128)(2,1)S(1)} %get-tuple-element.7), channel_id=1, source_target_pairs={{1,2},{3,4},{5,6},{7,8},{9,10},{11,12},{13,14},{2,1},{4,3},{6,5},{... | collective-permute-start | bytes 24584 | tf_op jit(solution)/shard_map/ppermute | solution.py:188
  2.0 5.3 %collective-permute-start.2 = (bf16[8,512]{1,0:T(8,128)(2,1)S(1)}, bf16[8,512]{1,0:T(8,128)(2,1)S(1)}, u32[]{:S(2)}, u32[]{:S(2)}) collective-permute-start(bf16[8,512]{1,0:T(8,128)(2,1)S(1)} %get-tuple-element.8), channel_id=1, source_target_pairs={{0,1},{1,0},{2,3},{3,2},{4,5},{5,4},{6,7},{7,6},{8,9},{9,8},{10,11... | collective-permute-start | bytes 24584 | tf_op jit(solution)/shard_map/ppermute | solution.py:187
  7.3 0.0 copy-start.2
  7.3 2.2 %fusion = bf16[1024,512]{0,1:T(8,128)(2,1)S(1)} fusion(bf16[512,512]{1,0:T(8,128)(2,1)} %constant.31.clone.refs_4_, bf16[1024,512]{1,0:T(8,128)(2,1)} %bitcast.19), kind=kOutput, calls=%fused_computation.2 | convolution fusion | flops 537395200 | bytes 2621440 | tf_op jit(solution)/shard_map/dot_general | solution.py:204
  9.5 1.3 %copy.10 = bf16[1024,512]{1,0:T(8,128)(2,1)} copy(bf16[1024,512]{0,1:T(8,128)(2,1)S(1)} %fusion) | data formatting | bytes 2097152 | tf_op jit(solution)/shard_map/convert_element_type | solution.py:204
  10.9 0.0 collective-permute-done.1
  10.9 0.0 collective-permute-done.2
  10.9 0.0 copy-start
  10.9 0.1 collective-permute-start.3
  11.0 0.0 collective-permute-done
  11.0 0.0 copy-done.2
  11.0 0.8 %fusion.1 = bf16[1024,512]{0,1:T(8,128)(2,1)S(1)} fusion(bf16[512,512]{1,0:T(8,128)(2,1)S(1)} %copy-done.2, bf16[1024,512]{1,0:T(8,128)(2,1)S(1)} %bitcast.20), kind=kOutput, calls=%fused_computation.3 | convolution fusion | flops 537395200 | bytes 2621440 | tf_op jit(solution)/shard_map/dot_general | solution.py:204
  11.8 1.3 %copy.11 = bf16[1024,512]{1,0:T(8,128)(2,1)} copy(bf16[1024,512]{0,1:T(8,128)(2,1)S(1)} %fusion.1) | data formatting | bytes 2097152 | tf_op jit(solution)/shard_map/convert_element_type | solution.py:204
  13.1 0.0 copy-done
  13.1 0.0 collective-permute-done.3.refs_3_
  13.1 0.0 copy-start.1
  13.1 0.6 %copy-done.1 = bf16[16,512]{1,0:T(8,128)(2,1)} copy-done((bf16[16,512]{1,0:T(8,128)(2,1)}, bf16[16,512]{1,0:T(8,128)(2,1)S(1)}, u32[]{:S(2)}) %copy-start.1) | copy-done | bytes 16408
  13.7 21.2 %shard_map.91 = bf16[8,9,128,512]{3,2,1,0:T(8,128)(2,1)} custom-call(s32[1]{0:T(128)} %bitcast.block, s32[16]{0:T(128)} %count.1, s32[16,9]{1,0:T(8,128)} %partner.1, s32[8,9]{1,0:T(8,128)} %low.1, s32[8,9]{1,0:T(8,128)} %high.1, bf16[8,128,512]{2,1,0:T(8,128)(2,1)} %bitcast.17, bf16[8,128,512]{2,1,0:T(8,128)(2,1)} %bitcast.18, bf16[16,512]{1,0:T(8,128)(2,1)} %copy-done, ...), custom_call_target="tpu_custom_call" | custom-call | flops 9663676416 | bytes 9437184 | tf_op jit(solution)/shard_map/pallas_call | solution.py:163
  (3 shorter events, 0.0 us)
Async XLA Ops:
  0.0 11.0 %collective-permute-start = (bf16[8,128,512]{2,1,0:T(8,128)(2,1)}, bf16[8,128,512]{2,1,0:T(8,128)(2,1)S(1)}, u32[]{:S(2)}, u32[]{:S(2)}) collective-permute-start(bf16[8,128,512]{2,1,0:T(8,128)(2,1)} %param.9), channel_id=1, source_target_pairs={{16,0},{0,16},{17,1},{1,17},{18,2},{2,18},{19,3},{3,19},{20,4},{4,... | collective-permute-start | bytes 3145736 | tf_op jit(solution)/shard_map/ppermute | solution.py:198
  1.4 9.5 %collective-permute-start.1 = (bf16[8,512]{1,0:T(8,128)(2,1)S(1)}, bf16[8,512]{1,0:T(8,128)(2,1)S(1)}, u32[]{:S(2)}, u32[]{:S(2)}) collective-permute-start(bf16[8,512]{1,0:T(8,128)(2,1)S(1)} %get-tuple-element.7), channel_id=1, source_target_pairs={{1,2},{3,4},{5,6},{7,8},{9,10},{11,12},{13,14},{2,1},{4,3},{6,5},{... | collective-permute-start | bytes 24584 | tf_op jit(solution)/shard_map/ppermute | solution.py:188
  2.0 8.8 %collective-permute-start.2 = (bf16[8,512]{1,0:T(8,128)(2,1)S(1)}, bf16[8,512]{1,0:T(8,128)(2,1)S(1)}, u32[]{:S(2)}, u32[]{:S(2)}) collective-permute-start(bf16[8,512]{1,0:T(8,128)(2,1)S(1)} %get-tuple-element.8), channel_id=1, source_target_pairs={{0,1},{1,0},{2,3},{3,2},{4,5},{5,4},{6,7},{7,6},{8,9},{9,8},{10,11... | collective-permute-start | bytes 24584 | tf_op jit(solution)/shard_map/ppermute | solution.py:187
  7.3 3.7 %copy-start.2 = (bf16[512,512]{1,0:T(8,128)(2,1)S(1)}, bf16[512,512]{1,0:T(8,128)(2,1)}, u32[]{:S(2)}) copy-start(bf16[512,512]{1,0:T(8,128)(2,1)} %constant.31.clone.refs_4_) | copy-start | bytes 1572868
  10.9 2.2 %copy-start = (bf16[16,512]{1,0:T(8,128)(2,1)}, bf16[16,512]{1,0:T(8,128)(2,1)S(1)}, u32[]{:S(2)}) copy-start(bf16[16,512]{1,0:T(8,128)(2,1)S(1)} %pad_maximum_fusion.refs_2_) | copy-start | bytes 49156
  10.9 2.2 %collective-permute-start.3 = (bf16[16,512]{1,0:T(8,128)(2,1)S(1)}, bf16[16,512]{1,0:T(8,128)(2,1)S(1)}, u32[]{:S(2)}, u32[]{:S(2)}) collective-permute-start(bf16[16,512]{1,0:T(8,128)(2,1)S(1)} %pad_maximum_fusion.refs_2_), channel_id=1, source_target_pairs={{16,0},{0,16},{17,1},{1,17},{18,2},{2,18},{19,3},{3,19},{20,4},{4,... | collective-permute-start | bytes 49160 | tf_op jit(solution)/shard_map/ppermute | solution.py:198
  13.1 0.6 %copy-start.1 = (bf16[16,512]{1,0:T(8,128)(2,1)}, bf16[16,512]{1,0:T(8,128)(2,1)S(1)}, u32[]{:S(2)}) copy-start(bf16[16,512]{1,0:T(8,128)(2,1)S(1)} %collective-permute-done.3.refs_3_) | copy-start | bytes 49156

commit v2 on v1

--- a/solution.py
+++ b/solution.py
@@ -6,6 +6,7 @@
 import numpy as np
 from jax import lax
 from jax.experimental import pallas as pl
+from jax.experimental.layout import Layout, with_layout_constraint
 from jax.experimental.pallas import tpu as pltpu
 from jax.sharding import PartitionSpec as P
 
@@ -78,12 +79,12 @@
         b = (spectra[away * dates + second % dates].reshape(tiled) * mask).reshape(ext, cols)
         return [a, b]
 
-    def filter_date(date, ring):
-        x = jnp.concatenate([m for slot in range(slots) for m in masked(date, slot)], 0)
+    def filter_date(date, ring, group):
+        x = jnp.concatenate([m for slot in group for m in masked(date, slot)], 0)
         e = dot(x[:, :bins], even)
         o = dot(x[:, bins:], odd)
-        for slot in range(slots):
-            r = slice(2 * slot * ext, (2 * slot + 2) * ext)
+        for i, slot in enumerate(group):
+            r = slice(2 * i * ext, (2 * i + 2) * ext)
             for c, v in enumerate(((e[r] + o[r]).astype(BF), (e[r] - o[r]).astype(BF))):
                 a_re, a_im, b_re, b_im = v[:ext, :half], v[:ext, half:], v[ext:, :half], v[ext:, half:]
                 fields = (
@@ -95,25 +96,21 @@
                 for q, field in enumerate(fields):
                     sums[ring, slot, q * ext : (q + 1) * ext, c * half : (c + 1) * half] = field
 
-    def look_date(ring):
-        cut = slots // 2
-        groups = [list(range(cut)), list(range(cut, slots))]
-        summed = []
-        for group in groups:
-            if group:
-                y = dot(jnp.concatenate([sums[ring, slot] for slot in group], 0), window)
-                summed += [y[4 * i * ext : 4 * (i + 1) * ext] for i in range(len(group))]
-        for slot in range(slots):
+    def look_date(ring, group):
+        flat = jnp.concatenate([sums[ring, slot] for slot in group], 0)
+        cut = flat.shape[0] // (2 * TILE) * TILE
+        summed = jnp.concatenate([dot(flat[:cut], window), dot(flat[cut:], window)], 0)
+        for i, slot in enumerate(group):
             looked = []
             for q in range(4):
                 parts = []
                 for c in range(2):
-                    v = summed[slot][q * ext : (q + 1) * ext, c * half : (c + 1) * half]
+                    v = summed[(4 * i + q) * ext : (4 * i + q + 1) * ext, c * half : (c + 1) * half]
                     held = across.at[slot, 2 * q + c]
                     held[0:SUB] = v[ext - SUB :]
                     held[SUB:ext] = v[: ext - SUB]
                     parts.append(
-                        held[SUB - 1 : SUB - 1 + rows] + held[SUB : SUB + rows] + held[SUB + 1 : SUB + 1 + rows]
+                        held[SUB - 1 : SUB - 1 + rows] + v[:rows] + held[SUB + 1 : SUB + 1 + rows]
                     )
                 looked.append(jnp.concatenate(parts, 1))
             scale = lax.rsqrt(jnp.maximum(looked[2], 1.0) * jnp.maximum(looked[3], 1.0))
@@ -125,7 +122,11 @@
 
     for k in range(blocks):
         main_copy(k).wait()
-    filter_date(0, 0)
+    parts_of_date = 1
+    groups = [list(range(slots * g // parts_of_date, slots * (g + 1) // parts_of_date)) for g in range(parts_of_date)]
+    groups = [g for g in groups if g]
+    for group in groups:
+        filter_date(0, 0, group)
 
     def body(date, _):
         now = lax.rem(date, 2)
@@ -135,8 +136,9 @@
         def _():
             send(date - 3, last).wait()
 
-        look_date(last)
-        filter_date(date, now)
+        for group in groups:
+            look_date(last, group)
+            filter_date(date, now, group)
         send(date - 1, last).start()
         return 0
 
@@ -144,7 +146,8 @@
     end = (dates - 1) % 2
     if dates >= 3:
         send(dates - 3, end).wait()
-    look_date(end)
+    for group in groups:
+        look_date(end, group)
     send(dates - 1, end).start()
     if dates >= 2:
         send(dates - 2, 1 - end).wait()
@@ -174,7 +177,7 @@
             pltpu.SemaphoreType.DMA((2,)),
         ],
         cost_estimate=pl.CostEstimate(flops=work * cols * 4, bytes_accessed=work * 2, transcendentals=work // 2),
-        compiler_params=pltpu.CompilerParams(vmem_limit_bytes=58 * 2**20),
+        compiler_params=pltpu.CompilerParams(vmem_limit_bytes=53 * 2**20),
     )(block, count, partner, low, high, *mains, *edges, *tables)
 
 
@@ -202,6 +205,7 @@
     for k in range(blocks):
         strip = from_ahead(acquisitions, k).reshape(dates * rows, cols)
         spectrum = jnp.dot(strip, tables[0], preferred_element_type=F32).astype(BF)
+        spectrum = with_layout_constraint(spectrum, Layout(major_to_minor=(0, 1)))
         mains.append(spectrum.reshape(dates, rows, cols))
     edges = [from_ahead(edge, k) for k in range(blocks)]
     block = lax.axis_index("date").reshape(1).astype(jnp.int32)

time: 35.2 us -> 33.4 us (0.949)
  local copies, waits for them, and re-layouts: 4.15 us -> 0.94 us
  matrix products: 2.96 us -> 4.75 us
  Pallas kernels: 21.2 us -> 20.8 us
    convert_element_type x2 -> x0, local copies, waits for them, and re-layouts: 2.64 us -> none  [local(): spectrum = jnp.dot(strip, tables[0], preferred_element_type=F32).astype(BF)]
    dot_general x2, matrix products: 2.96 us -> 4.75 us  [local(): spectrum = jnp.dot(strip, tables[0], preferred_element_type=F32).astype(BF)]
    unnamed x6 -> x16, local copies, waits for them, and re-layouts: 0.61 us -> 0.04 us
    pallas_call x1, Pallas kernels: 21.2 us -> 20.8 us  [pairs(): pl.pallas_call(functools.partial(pairs_kernel, blocks=blocks), in_specs=[...]
  transfers between devices with their start and end apart: 4 -> 4, of which waited for: 0 -> 0; matrix products, arithmetic and copies ran while one was open for 19% -> 17% of each run, Pallas kernels for 0% -> 0%
where the time goes in v2:
time: 33.4 us; the launch traced here: 33.2 us
  Pallas kernels  20.8 us (62%)
  starting transfers between devices  6.54 us (20%)
  matrix products  4.75 us (14%)
  local copies, waits for them, and re-layouts  0.94 us (3%)
    pallas_call x1, Pallas kernels, pairs(): pl.pallas_call(functools.partial(pairs_kernel, blocks=blocks), in_specs=[...  20.8 us
    ppermute x1, starting transfers between devices, edge_rows(): from_inner = lax.ppermute(jnp.where(even, last, first), 'space', inner)  5.35 us
    dot_general x2, matrix products, local(): spectrum = jnp.dot(strip, tables[0], preferred_element_type=F32).astype(BF)  4.75 us
    slice x1, local copies, waits for them, and re-layouts, edge_rows(): first, last = (strips[:, 0, :], strips[:, -1, :])  0.9 us
  transfers between devices with their start and end apart: 4, of which 0 were waited for; matrix products, arithmetic and copies ran while one was open for 17% of the time, Pallas kernels for 0%

profile of v2, /device:TPU:0, one launch (start us, length us, event | category | flops | bytes accessed | tf_op | source)
XLA Modules:
  0.0 33.2 jit_solution(365074783015076800)
XLA Ops:
  0.0 0.0 copy-start.4
  0.0 0.5 %collective-permute-start = (bf16[8,128,512]{2,1,0:T(8,128)(2,1)}, bf16[8,128,512]{2,1,0:T(8,128)(2,1)S(1)}, u32[]{:S(2)}, u32[]{:S(2)}) collective-permute-start(bf16[8,128,512]{2,1,0:T(8,128)(2,1)} %param.9), channel_id=1, source_target_pairs={{16,0},{0,16},{17,1},{1,17},{18,2},{2,18},{19,3},{3,19},{20,4},{4,... | collective-permute-start | bytes 3145736 | tf_op jit(solution)/shard_map/ppermute | solution.py:201
  0.5 0.9 %fusion = (bf16[8,1,512]{2,1,0:T(2,128)(2,1)S(1)}, bf16[8,1,512]{2,1,0:T(2,128)(2,1)S(1)}) fusion(bf16[8,128,512]{2,1,0:T(8,128)(2,1)} %param.9), kind=kLoop, calls=%fused_computation.7 | loop fusion | bytes 32768 | tf_op jit(solution)/shard_map/slice | solution.py:187
  1.4 0.7 %collective-permute-start.1 = (bf16[8,512]{1,0:T(8,128)(2,1)S(1)}, bf16[8,512]{1,0:T(8,128)(2,1)S(1)}, u32[]{:S(2)}, u32[]{:S(2)}) collective-permute-start(bf16[8,512]{1,0:T(8,128)(2,1)S(1)} %get-tuple-element.7), channel_id=1, source_target_pairs={{1,2},{3,4},{5,6},{7,8},{9,10},{11,12},{13,14},{2,1},{4,3},{6,5},{... | collective-permute-start | bytes 24584 | tf_op jit(solution)/shard_map/ppermute | solution.py:191
  2.0 5.3 %collective-permute-start.2 = (bf16[8,512]{1,0:T(8,128)(2,1)S(1)}, bf16[8,512]{1,0:T(8,128)(2,1)S(1)}, u32[]{:S(2)}, u32[]{:S(2)}) collective-permute-start(bf16[8,512]{1,0:T(8,128)(2,1)S(1)} %get-tuple-element.8), channel_id=1, source_target_pairs={{0,1},{1,0},{2,3},{3,2},{4,5},{5,4},{6,7},{7,6},{8,9},{9,8},{10,11... | collective-permute-start | bytes 24584 | tf_op jit(solution)/shard_map/ppermute | solution.py:190
  7.4 3.0 %convolution_convert_fusion.1 = bf16[512,1024]{0,1:T(8,128)(2,1)} fusion(bf16[1024,512]{1,0:T(8,128)(2,1)} %bitcast.17, bf16[512,512]{1,0:T(8,128)(2,1)} %constant.31.clone.refs_4_), kind=kOutput, calls=%fused_computation.1 | convolution fusion | flops 537395200 | bytes 2621440 | tf_op jit(solution)/shard_map/dot_general | solution.py:207
  10.5 0.0 copy-start.5
  10.5 0.0 copy-start.6
  10.5 0.0 copy-start.7
  10.5 0.0 collective-permute-done.1
  10.5 0.0 collective-permute-done.2
  10.5 0.1 collective-permute-start.3
  10.6 0.0 collective-permute-done
  10.6 0.0 copy-done.4
  10.6 1.7 %convolution_convert_fusion = bf16[512,1024]{0,1:T(8,128)(2,1)} fusion(bf16[1024,512]{1,0:T(8,128)(2,1)S(1)} %bitcast.18, bf16[512,512]{1,0:T(8,128)(2,1)S(1)} %copy-done.4), kind=kOutput, calls=%fused_computation | convolution fusion | flops 537395200 | bytes 2621440 | tf_op jit(solution)/shard_map/dot_general | solution.py:207
  12.3 0.0 collective-permute-done.3.refs_3_
  12.4 0.0 copy-done
  12.4 0.0 copy-done.1
  12.4 0.0 copy-done.2
  12.4 0.0 copy-done.3
  12.4 0.0 copy-done.5
  12.4 0.0 copy-done.6
  12.4 0.0 copy-done.7
  12.4 20.8 %shard_map.91 = bf16[8,9,128,512]{3,2,1,0:T(8,128)(2,1)} custom-call(s32[1]{0:T(128)} %bitcast.block, s32[16]{0:T(128)S(1)} %copy-done.3, s32[16,9]{1,0:T(8,128)S(1)} %copy-done, s32[8,9]{1,0:T(8,128)S(1)} %copy-done.1, s32[8,9]{1,0:T(8,128)S(1)} %copy-done.2, bf16[8,128,512]{2,1,0:T(8,128)(2,1)} %bitcast.19, bf16[8,128,512]{2,1,0:T(8,128)(2,1)} %bitcast.20, ...), custom_call_target="tpu_custom_call" | custom-call | flops 9663676416 | bytes 9437184 | tf_op jit(solution)/shard_map/pallas_call | solution.py:166
  (7 shorter events, 0.0 us)
Async XLA Ops:
  0.0 10.6 %copy-start.4 = (bf16[512,512]{1,0:T(8,128)(2,1)S(1)}, bf16[512,512]{1,0:T(8,128)(2,1)}, u32[]{:S(2)}) copy-start(bf16[512,512]{1,0:T(8,128)(2,1)} %constant.31.clone.refs_4_) | copy-start | bytes 1572868
  0.0 10.6 %collective-permute-start = (bf16[8,128,512]{2,1,0:T(8,128)(2,1)}, bf16[8,128,512]{2,1,0:T(8,128)(2,1)S(1)}, u32[]{:S(2)}, u32[]{:S(2)}) collective-permute-start(bf16[8,128,512]{2,1,0:T(8,128)(2,1)} %param.9), channel_id=1, source_target_pairs={{16,0},{0,16},{17,1},{1,17},{18,2},{2,18},{19,3},{3,19},{20,4},{4,... | collective-permute-start | bytes 3145736 | tf_op jit(solution)/shard_map/ppermute | solution.py:201
  1.4 9.1 %collective-permute-start.1 = (bf16[8,512]{1,0:T(8,128)(2,1)S(1)}, bf16[8,512]{1,0:T(8,128)(2,1)S(1)}, u32[]{:S(2)}, u32[]{:S(2)}) collective-permute-start(bf16[8,512]{1,0:T(8,128)(2,1)S(1)} %get-tuple-element.7), channel_id=1, source_target_pairs={{1,2},{3,4},{5,6},{7,8},{9,10},{11,12},{13,14},{2,1},{4,3},{6,5},{... | collective-permute-start | bytes 24584 | tf_op jit(solution)/shard_map/ppermute | solution.py:191
  2.0 8.5 %collective-permute-start.2 = (bf16[8,512]{1,0:T(8,128)(2,1)S(1)}, bf16[8,512]{1,0:T(8,128)(2,1)S(1)}, u32[]{:S(2)}, u32[]{:S(2)}) collective-permute-start(bf16[8,512]{1,0:T(8,128)(2,1)S(1)} %get-tuple-element.8), channel_id=1, source_target_pairs={{0,1},{1,0},{2,3},{3,2},{4,5},{5,4},{6,7},{7,6},{8,9},{9,8},{10,11... | collective-permute-start | bytes 24584 | tf_op jit(solution)/shard_map/ppermute | solution.py:190
  10.4 1.9 %copy-start = (s32[16,9]{1,0:T(8,128)S(1)}, s32[16,9]{1,0:T(8,128)}, u32[]{:S(2)}) copy-start(s32[16,9]{1,0:T(8,128)} %partner.1) | copy-start | bytes 1732
  10.4 1.9 %copy-start.1 = (s32[8,9]{1,0:T(8,128)S(1)}, s32[8,9]{1,0:T(8,128)}, u32[]{:S(2)}) copy-start(s32[8,9]{1,0:T(8,128)} %low.1) | copy-start | bytes 868
  10.4 1.9 %copy-start.2 = (s32[8,9]{1,0:T(8,128)S(1)}, s32[8,9]{1,0:T(8,128)}, u32[]{:S(2)}) copy-start(s32[8,9]{1,0:T(8,128)} %high.1) | copy-start | bytes 868
  10.4 1.9 %copy-start.3 = (s32[16]{0:T(128)S(1)}, s32[16]{0:T(128)}, u32[]{:S(2)}) copy-start(s32[16]{0:T(128)} %count.1) | copy-start | bytes 196
  10.5 1.9 %copy-start.5 = (bf16[256,256]{1,0:T(8,128)(2,1)S(1)}, bf16[256,256]{1,0:T(8,128)(2,1)}, u32[]{:S(2)}) copy-start(bf16[256,256]{1,0:T(8,128)(2,1)} %constant.34.clone.refs_7_) | copy-start | bytes 393220
  10.5 1.9 %copy-start.6 = (bf16[256,256]{1,0:T(8,128)(2,1)S(1)}, bf16[256,256]{1,0:T(8,128)(2,1)}, u32[]{:S(2)}) copy-start(bf16[256,256]{1,0:T(8,128)(2,1)} %constant.33.clone.refs_6_) | copy-start | bytes 393220
  10.5 1.9 %copy-start.7 = (bf16[256,256]{1,0:T(8,128)(2,1)S(1)}, bf16[256,256]{1,0:T(8,128)(2,1)}, u32[]{:S(2)}) copy-start(bf16[256,256]{1,0:T(8,128)(2,1)} %constant.32.clone.refs_5_) | copy-start | bytes 393220
  10.5 1.8 %collective-permute-start.3 = (bf16[16,512]{1,0:T(8,128)(2,1)S(1)}, bf16[16,512]{1,0:T(8,128)(2,1)S(1)}, u32[]{:S(2)}, u32[]{:S(2)}) collective-permute-start(bf16[16,512]{1,0:T(8,128)(2,1)S(1)} %pad_maximum_fusion.refs_2_), channel_id=1, source_target_pairs={{16,0},{0,16},{17,1},{1,17},{18,2},{2,18},{19,3},{3,19},{20,4},{4,... | collective-permute-start | bytes 49160 | tf_op jit(solution)/shard_map/ppermute | solution.py:201

commit v3 on v2

--- a/solution.py
+++ b/solution.py
@@ -46,12 +46,14 @@
     half = bins // 2
     here = block[0]
 
-    def main_copy(k):
-        place = spectra.at[pl.ds(k * dates, dates), pl.ds(0, rows)]
-        return pltpu.make_async_copy(mains[k], place, main_sem.at[k])
-
-    for k in range(blocks):
-        main_copy(k).start()
+    def main_copy(k, first, last, sem):
+        place = spectra.at[pl.ds(k * dates + first, last - first), pl.ds(0, rows)]
+        return pltpu.make_async_copy(mains[k].at[pl.ds(first, last - first)], place, main_sem.at[sem])
+
+    early = [main_copy(k, 0, dates, k) for k in range(1, blocks)] + [main_copy(0, 0, 1, 0)]
+    later = [main_copy(0, 1, dates, blocks)] if dates > 1 else []
+    for copy in early + later:
+        copy.start()
 
     tile_row = lax.broadcasted_iota(jnp.int32, (TILE, cols), 0)
     for k in range(blocks):
@@ -96,7 +98,7 @@
                 for q, field in enumerate(fields):
                     sums[ring, slot, q * ext : (q + 1) * ext, c * half : (c + 1) * half] = field
 
-    def look_date(ring, group):
+    def look_date(ring, group, then=None):
         flat = jnp.concatenate([sums[ring, slot] for slot in group], 0)
         cut = flat.shape[0] // (2 * TILE) * TILE
         summed = jnp.concatenate([dot(flat[:cut], window), dot(flat[cut:], window)], 0)
@@ -116,17 +118,21 @@
             scale = lax.rsqrt(jnp.maximum(looked[2], 1.0) * jnp.maximum(looked[3], 1.0))
             ready[ring, slot, :, :bins] = (looked[0] * scale).astype(BF)
             ready[ring, slot, :, bins:] = (looked[1] * scale).astype(BF)
+            if then is not None:
+                then(slot)
 
     def send(date, ring):
         return pltpu.make_async_copy(ready.at[ring], out.at[date], out_sem.at[ring])
 
-    for k in range(blocks):
-        main_copy(k).wait()
+    for copy in early:
+        copy.wait()
     parts_of_date = 1
     groups = [list(range(slots * g // parts_of_date, slots * (g + 1) // parts_of_date)) for g in range(parts_of_date)]
     groups = [g for g in groups if g]
     for group in groups:
         filter_date(0, 0, group)
+    for copy in later:
+        copy.wait()
 
     def body(date, _):
         now = lax.rem(date, 2)
@@ -144,11 +150,14 @@
 
     lax.fori_loop(1, dates, body, 0)
     end = (dates - 1) % 2
+
+    def send_slot(slot):
+        pltpu.make_async_copy(ready.at[end, slot], out.at[dates - 1, slot], out_sem.at[end]).start()
+
     if dates >= 3:
         send(dates - 3, end).wait()
     for group in groups:
-        look_date(end, group)
-    send(dates - 1, end).start()
+        look_date(end, group, send_slot)
     if dates >= 2:
         send(dates - 2, 1 - end).wait()
     send(dates - 1, end).wait()
@@ -173,7 +182,7 @@
             pltpu.VMEM((2, slots, 4 * ext, cols // 2), BF),
             pltpu.VMEM((slots, 8, ext, cols // 4), F32),
             pltpu.VMEM((2, slots, rows, cols), BF),
-            pltpu.SemaphoreType.DMA((blocks,)),
+            pltpu.SemaphoreType.DMA((blocks + 1,)),
             pltpu.SemaphoreType.DMA((2,)),
         ],
         cost_estimate=pl.CostEstimate(flops=work * cols * 4, bytes_accessed=work * 2, transcendentals=work // 2),
@@ -189,7 +198,8 @@
     outer = [(i, i + 1) for i in range(1, n - 1, 2)] + [(i + 1, i) for i in range(1, n - 1, 2)]
     from_inner = lax.ppermute(jnp.where(even, last, first), "space", inner)
     from_outer = lax.ppermute(jnp.where(even, first, last), "space", outer)
-    return jnp.concatenate([jnp.where(even, from_outer, from_inner), jnp.where(even, from_inner, from_outer)], 0)
+    odd = jnp.logical_not(even)
+    return jnp.concatenate([jnp.where(odd, from_inner, from_outer), jnp.where(odd, from_outer, from_inner)], 0)
 
 
 def local(acquisitions, partner, pair_count, band_low, band_high):

time: 33.4 us -> 32.9 us (0.985)
  the two profiles are of different devices: /device:TPU:0 before, /device:TPU:9 now
where the time goes in v3:
time: 32.9 us; the launch traced here: 32.7 us
  Pallas kernels  20.3 us (62%)
  starting transfers between devices  6.5 us (20%)
  matrix products  4.76 us (14%)
  local copies, waits for them, and re-layouts  0.94 us (3%)
    pallas_call x1, Pallas kernels, pairs(): pl.pallas_call(functools.partial(pairs_kernel, blocks=blocks), in_specs=[...  20.3 us
    dot_general x2, matrix products, local(): spectrum = jnp.dot(strip, tables[0], preferred_element_type=F32).astype(BF)  4.76 us
    ppermute x1, starting transfers between devices, edge_rows(): from_outer = lax.ppermute(jnp.where(even, first, last), 'space', outer)  2.99 us
    ppermute x2, starting transfers between devices, from_ahead(): lax.ppermute(x, 'date', [((i + k) % blocks, i) for i in range(blocks)])  2.23 us
    ppermute x1, starting transfers between devices, edge_rows(): from_inner = lax.ppermute(jnp.where(even, last, first), 'space', inner)  1.28 us
    slice x1, local copies, waits for them, and re-layouts, edge_rows(): first, last = (strips[:, 0, :], strips[:, -1, :])  0.9 us
  transfers between devices with their start and end apart: 4, of which 1 were waited for; matrix products, arithmetic and copies ran while one was open for 17% of the time, Pallas kernels for 0%

profile of v3, /device:TPU:9, one launch (start us, length us, event | category | flops | bytes accessed | tf_op | source)
XLA Modules:
  0.0 32.7 jit_solution(6388729832529307177)
XLA Ops:
  0.0 0.0 copy-start.4
  0.0 0.7 %collective-permute-start = (bf16[8,128,512]{2,1,0:T(8,128)(2,1)}, bf16[8,128,512]{2,1,0:T(8,128)(2,1)S(1)}, u32[]{:S(2)}, u32[]{:S(2)}) collective-permute-start(bf16[8,128,512]{2,1,0:T(8,128)(2,1)} %param.9), channel_id=1, source_target_pairs={{16,0},{0,16},{17,1},{1,17},{18,2},{2,18},{19,3},{3,19},{20,4},{4,... | collective-permute-start | bytes 3145736 | tf_op jit(solution)/shard_map/ppermute | solution.py:211
  0.7 0.9 %fusion = (bf16[8,1,512]{2,1,0:T(2,128)(2,1)S(1)}, bf16[8,1,512]{2,1,0:T(2,128)(2,1)S(1)}) fusion(bf16[8,128,512]{2,1,0:T(8,128)(2,1)} %param.9), kind=kLoop, calls=%fused_computation.7 | loop fusion | bytes 32768 | tf_op jit(solution)/shard_map/slice | solution.py:196
  1.6 1.3 %collective-permute-start.1 = (bf16[8,512]{1,0:T(8,128)(2,1)S(1)}, bf16[8,512]{1,0:T(8,128)(2,1)S(1)}, u32[]{:S(2)}, u32[]{:S(2)}) collective-permute-start(bf16[8,512]{1,0:T(8,128)(2,1)S(1)} %get-tuple-element.7), channel_id=1, source_target_pairs={{0,1},{1,0},{2,3},{3,2},{4,5},{5,4},{6,7},{7,6},{8,9},{9,8},{10,11... | collective-permute-start | bytes 24584 | tf_op jit(solution)/shard_map/ppermute | solution.py:199
  2.9 3.0 %collective-permute-start.2 = (bf16[8,512]{1,0:T(8,128)(2,1)S(1)}, bf16[8,512]{1,0:T(8,128)(2,1)S(1)}, u32[]{:S(2)}, u32[]{:S(2)}) collective-permute-start(bf16[8,512]{1,0:T(8,128)(2,1)S(1)} %get-tuple-element.8), channel_id=1, source_target_pairs={{1,2},{3,4},{5,6},{7,8},{9,10},{11,12},{13,14},{2,1},{4,3},{6,5},{... | collective-permute-start | bytes 24584 | tf_op jit(solution)/shard_map/ppermute | solution.py:200
  5.9 3.0 %convolution_convert_fusion.1 = bf16[512,1024]{0,1:T(8,128)(2,1)} fusion(bf16[1024,512]{1,0:T(8,128)(2,1)} %bitcast.17, bf16[512,512]{1,0:T(8,128)(2,1)} %constant.31.clone.refs_4_), kind=kOutput, calls=%fused_computation.1 | convolution fusion | flops 537395200 | bytes 2621440 | tf_op jit(solution)/shard_map/dot_general | solution.py:217
  8.9 0.0 copy-start.5
  8.9 0.0 copy-start.6
  9.0 0.0 copy-start.7
  9.0 0.0 collective-permute-done.1
  9.0 0.1 collective-permute-done.2
  9.1 1.6 %collective-permute-start.3 = (bf16[16,512]{1,0:T(8,128)(2,1)S(1)}, bf16[16,512]{1,0:T(8,128)(2,1)S(1)}, u32[]{:S(2)}, u32[]{:S(2)}) collective-permute-start(bf16[16,512]{1,0:T(8,128)(2,1)S(1)} %pad_maximum_fusion.refs_2_), channel_id=1, source_target_pairs={{16,0},{0,16},{17,1},{1,17},{18,2},{2,18},{19,3},{3,19},{20,4},{4,... | collective-permute-start | bytes 49160 | tf_op jit(solution)/shard_map/ppermute | solution.py:211
  10.6 0.0 collective-permute-done
  10.6 0.0 copy-done.4
  10.6 1.7 %convolution_convert_fusion = bf16[512,1024]{0,1:T(8,128)(2,1)} fusion(bf16[1024,512]{1,0:T(8,128)(2,1)S(1)} %bitcast.18, bf16[512,512]{1,0:T(8,128)(2,1)S(1)} %copy-done.4), kind=kOutput, calls=%fused_computation | convolution fusion | flops 537395200 | bytes 2621440 | tf_op jit(solution)/shard_map/dot_general | solution.py:217
  12.3 0.0 collective-permute-done.3.refs_3_
  12.3 0.0 copy-done
  12.3 0.0 copy-done.1
  12.3 0.0 copy-done.2
  12.4 0.0 copy-done.3
  12.4 0.0 copy-done.5
  12.4 0.0 copy-done.6
  12.4 0.0 copy-done.7
  12.4 20.3 %shard_map.91 = bf16[8,9,128,512]{3,2,1,0:T(8,128)(2,1)} custom-call(s32[1]{0:T(128)} %bitcast.block, s32[16]{0:T(128)S(1)} %copy-done.3, s32[16,9]{1,0:T(8,128)S(1)} %copy-done, s32[8,9]{1,0:T(8,128)S(1)} %copy-done.1, s32[8,9]{1,0:T(8,128)S(1)} %copy-done.2, bf16[8,128,512]{2,1,0:T(8,128)(2,1)} %bitcast.19, bf16[8,128,512]{2,1,0:T(8,128)(2,1)} %bitcast.20, ...), custom_call_target="tpu_custom_call" | custom-call | flops 9663676416 | bytes 9437184 | tf_op jit(solution)/shard_map/pallas_call | solution.py:175
  (7 shorter events, 0.0 us)
Async XLA Ops:
  0.0 10.6 %copy-start.4 = (bf16[512,512]{1,0:T(8,128)(2,1)S(1)}, bf16[512,512]{1,0:T(8,128)(2,1)}, u32[]{:S(2)}) copy-start(bf16[512,512]{1,0:T(8,128)(2,1)} %constant.31.clone.refs_4_) | copy-start | bytes 1572868
  0.0 10.6 %collective-permute-start = (bf16[8,128,512]{2,1,0:T(8,128)(2,1)}, bf16[8,128,512]{2,1,0:T(8,128)(2,1)S(1)}, u32[]{:S(2)}, u32[]{:S(2)}) collective-permute-start(bf16[8,128,512]{2,1,0:T(8,128)(2,1)} %param.9), channel_id=1, source_target_pairs={{16,0},{0,16},{17,1},{1,17},{18,2},{2,18},{19,3},{3,19},{20,4},{4,... | collective-permute-start | bytes 3145736 | tf_op jit(solution)/shard_map/ppermute | solution.py:211
  1.6 7.4 %collective-permute-start.1 = (bf16[8,512]{1,0:T(8,128)(2,1)S(1)}, bf16[8,512]{1,0:T(8,128)(2,1)S(1)}, u32[]{:S(2)}, u32[]{:S(2)}) collective-permute-start(bf16[8,512]{1,0:T(8,128)(2,1)S(1)} %get-tuple-element.7), channel_id=1, source_target_pairs={{0,1},{1,0},{2,3},{3,2},{4,5},{5,4},{6,7},{7,6},{8,9},{9,8},{10,11... | collective-permute-start | bytes 24584 | tf_op jit(solution)/shard_map/ppermute | solution.py:199
  2.9 6.2 %collective-permute-start.2 = (bf16[8,512]{1,0:T(8,128)(2,1)S(1)}, bf16[8,512]{1,0:T(8,128)(2,1)S(1)}, u32[]{:S(2)}, u32[]{:S(2)}) collective-permute-start(bf16[8,512]{1,0:T(8,128)(2,1)S(1)} %get-tuple-element.8), channel_id=1, source_target_pairs={{1,2},{3,4},{5,6},{7,8},{9,10},{11,12},{13,14},{2,1},{4,3},{6,5},{... | collective-permute-start | bytes 24584 | tf_op jit(solution)/shard_map/ppermute | solution.py:200
  8.9 3.4 %copy-start = (s32[16,9]{1,0:T(8,128)S(1)}, s32[16,9]{1,0:T(8,128)}, u32[]{:S(2)}) copy-start(s32[16,9]{1,0:T(8,128)} %partner.1) | copy-start | bytes 1732
  8.9 3.4 %copy-start.1 = (s32[8,9]{1,0:T(8,128)S(1)}, s32[8,9]{1,0:T(8,128)}, u32[]{:S(2)}) copy-start(s32[8,9]{1,0:T(8,128)} %low.1) | copy-start | bytes 868
  8.9 3.4 %copy-start.2 = (s32[8,9]{1,0:T(8,128)S(1)}, s32[8,9]{1,0:T(8,128)}, u32[]{:S(2)}) copy-start(s32[8,9]{1,0:T(8,128)} %high.1) | copy-start | bytes 868
  8.9 3.4 %copy-start.3 = (s32[16]{0:T(128)S(1)}, s32[16]{0:T(128)}, u32[]{:S(2)}) copy-start(s32[16]{0:T(128)} %count.1) | copy-start | bytes 196
  8.9 3.4 %copy-start.5 = (bf16[256,256]{1,0:T(8,128)(2,1)S(1)}, bf16[256,256]{1,0:T(8,128)(2,1)}, u32[]{:S(2)}) copy-start(bf16[256,256]{1,0:T(8,128)(2,1)} %constant.34.clone.refs_7_) | copy-start | bytes 393220
  8.9 3.4 %copy-start.6 = (bf16[256,256]{1,0:T(8,128)(2,1)S(1)}, bf16[256,256]{1,0:T(8,128)(2,1)}, u32[]{:S(2)}) copy-start(bf16[256,256]{1,0:T(8,128)(2,1)} %constant.33.clone.refs_6_) | copy-start | bytes 393220
  9.0 3.4 %copy-start.7 = (bf16[256,256]{1,0:T(8,128)(2,1)S(1)}, bf16[256,256]{1,0:T(8,128)(2,1)}, u32[]{:S(2)}) copy-start(bf16[256,256]{1,0:T(8,128)(2,1)} %constant.32.clone.refs_5_) | copy-start | bytes 393220
  9.1 3.3 %collective-permute-start.3 = (bf16[16,512]{1,0:T(8,128)(2,1)S(1)}, bf16[16,512]{1,0:T(8,128)(2,1)S(1)}, u32[]{:S(2)}, u32[]{:S(2)}) collective-permute-start(bf16[16,512]{1,0:T(8,128)(2,1)S(1)} %pad_maximum_fusion.refs_2_), channel_id=1, source_target_pairs={{16,0},{0,16},{17,1},{1,17},{18,2},{2,18},{19,3},{3,19},{20,4},{4,... | collective-permute-start | bytes 49160 | tf_op jit(solution)/shard_map/ppermute | solution.py:211

commit v4 on v3

--- a/solution.py
+++ b/solution.py
@@ -111,9 +111,8 @@
                     held = across.at[slot, 2 * q + c]
                     held[0:SUB] = v[ext - SUB :]
                     held[SUB:ext] = v[: ext - SUB]
-                    parts.append(
-                        held[SUB - 1 : SUB - 1 + rows] + v[:rows] + held[SUB + 1 : SUB + 1 + rows]
-                    )
+                    up = pltpu.roll(v, 1, 0)[:rows] if q < 2 else held[SUB - 1 : SUB - 1 + rows]
+                    parts.append(up + v[:rows] + held[SUB + 1 : SUB + 1 + rows])
                 looked.append(jnp.concatenate(parts, 1))
             scale = lax.rsqrt(jnp.maximum(looked[2], 1.0) * jnp.maximum(looked[3], 1.0))
             ready[ring, slot, :, :bins] = (looked[0] * scale).astype(BF)
@@ -186,7 +185,7 @@
             pltpu.SemaphoreType.DMA((2,)),
         ],
         cost_estimate=pl.CostEstimate(flops=work * cols * 4, bytes_accessed=work * 2, transcendentals=work // 2),
-        compiler_params=pltpu.CompilerParams(vmem_limit_bytes=53 * 2**20),
+        compiler_params=pltpu.CompilerParams(vmem_limit_bytes=50 * 2**20),
     )(block, count, partner, low, high, *mains, *edges, *tables)
 
 

time: 32.9 us -> 31.3 us (0.951)
  the two profiles are of different devices: /device:TPU:9 before, /device:TPU:25 now
where the time goes in v4:
time: 31.3 us; the launch traced here: 31.1 us
  Pallas kernels  19.6 us (63%)
  starting transfers between devices  6.5 us (21%)
  matrix products  2.76 us (9%)
  waiting for transfers between devices  1.14 us (4%)
  local copies, waits for them, and re-layouts  0.95 us (3%)
    pallas_call x1, Pallas kernels, pairs(): pl.pallas_call(functools.partial(pairs_kernel, blocks=blocks), in_specs=[...  19.6 us
    ppermute x1, starting transfers between devices, edge_rows(): from_outer = lax.ppermute(jnp.where(even, first, last), 'space', outer)  2.99 us
    dot_general x2, matrix products, local(): spectrum = jnp.dot(strip, tables[0], preferred_element_type=F32).astype(BF)  2.76 us
    ppermute x2, starting transfers between devices, from_ahead(): lax.ppermute(x, 'date', [((i + k) % blocks, i) for i in range(blocks)])  2.23 us
    ppermute x1, starting transfers between devices, edge_rows(): from_inner = lax.ppermute(jnp.where(even, last, first), 'space', inner)  1.28 us
    ppermute x1, waiting for transfers between devices, edge_rows(): from_outer = lax.ppermute(jnp.where(even, first, last), 'space', outer)  1.01 us
    slice x1, local copies, waits for them, and re-layouts, edge_rows(): first, last = (strips[:, 0, :], strips[:, -1, :])  0.9 us
  transfers between devices with their start and end apart: 4, of which 2 were waited for; matrix products, arithmetic and copies ran while one was open for 12% of the time, Pallas kernels for 0%

profile of v4, /device:TPU:25, one launch (start us, length us, event | category | flops | bytes accessed | tf_op | source)
XLA Modules:
  0.0 31.1 jit_solution(13437667315706482443)
XLA Ops:
  0.0 0.7 %collective-permute-start = (bf16[8,128,512]{2,1,0:T(8,128)(2,1)}, bf16[8,128,512]{2,1,0:T(8,128)(2,1)S(1)}, u32[]{:S(2)}, u32[]{:S(2)}) collective-permute-start(bf16[8,128,512]{2,1,0:T(8,128)(2,1)} %param.9), channel_id=1, source_target_pairs={{16,0},{0,16},{17,1},{1,17},{18,2},{2,18},{19,3},{3,19},{20,4},{4,... | collective-permute-start | bytes 3145736 | tf_op jit(solution)/shard_map/ppermute | solution.py:210
  0.7 0.9 %fusion = (bf16[8,1,512]{2,1,0:T(2,128)(2,1)S(1)}, bf16[8,1,512]{2,1,0:T(2,128)(2,1)S(1)}) fusion(bf16[8,128,512]{2,1,0:T(8,128)(2,1)} %param.9), kind=kLoop, calls=%fused_computation.7 | loop fusion | bytes 32768 | tf_op jit(solution)/shard_map/slice | solution.py:195
  1.6 1.3 %collective-permute-start.1 = (bf16[8,512]{1,0:T(8,128)(2,1)S(1)}, bf16[8,512]{1,0:T(8,128)(2,1)S(1)}, u32[]{:S(2)}, u32[]{:S(2)}) collective-permute-start(bf16[8,512]{1,0:T(8,128)(2,1)S(1)} %get-tuple-element.7), channel_id=1, source_target_pairs={{0,1},{1,0},{2,3},{3,2},{4,5},{5,4},{6,7},{7,6},{8,9},{9,8},{10,11... | collective-permute-start | bytes 24584 | tf_op jit(solution)/shard_map/ppermute | solution.py:198
  2.9 3.0 %collective-permute-start.2 = (bf16[8,512]{1,0:T(8,128)(2,1)S(1)}, bf16[8,512]{1,0:T(8,128)(2,1)S(1)}, u32[]{:S(2)}, u32[]{:S(2)}) collective-permute-start(bf16[8,512]{1,0:T(8,128)(2,1)S(1)} %get-tuple-element.8), channel_id=1, source_target_pairs={{1,2},{3,4},{5,6},{7,8},{9,10},{11,12},{13,14},{2,1},{4,3},{6,5},{... | collective-permute-start | bytes 24584 | tf_op jit(solution)/shard_map/ppermute | solution.py:199
  5.9 2.1 %convolution_convert_fusion.1 = bf16[512,1024]{0,1:T(8,128)(2,1)S(1)} fusion(bf16[1024,512]{1,0:T(8,128)(2,1)} %bitcast.19, bf16[512,512]{1,0:T(8,128)(2,1)} %constant.31.clone.refs_4_), kind=kOutput, calls=%fused_computation.1 | convolution fusion | flops 537395200 | bytes 2621440 | tf_op jit(solution)/shard_map/dot_general | solution.py:216
  7.9 0.0 copy-start
  8.0 0.0 copy-start.1
  8.0 0.0 copy-start.2
  8.0 0.0 copy-start.3
  8.0 0.0 copy-start.5
  8.0 0.0 copy-start.6
  8.0 0.0 copy-start.7
  8.0 0.0 collective-permute-done.1
  8.0 1.0 %collective-permute-done.2 = bf16[8,512]{1,0:T(8,128)(2,1)S(1)} collective-permute-done((bf16[8,512]{1,0:T(8,128)(2,1)S(1)}, bf16[8,512]{1,0:T(8,128)(2,1)S(1)}, u32[]{:S(2)}, u32[]{:S(2)}) %collective-permute-start.2) | collective-permute-done | bytes 8224 | tf_op jit(solution)/shard_map/ppermute | solution.py:199
  9.1 1.6 %collective-permute-start.3 = (bf16[16,512]{1,0:T(8,128)(2,1)S(1)}, bf16[16,512]{1,0:T(8,128)(2,1)S(1)}, u32[]{:S(2)}, u32[]{:S(2)}) collective-permute-start(bf16[16,512]{1,0:T(8,128)(2,1)S(1)} %pad_maximum_fusion.refs_2_), channel_id=1, source_target_pairs={{16,0},{0,16},{17,1},{1,17},{18,2},{2,18},{19,3},{3,19},{20,4},{4,... | collective-permute-start | bytes 49160 | tf_op jit(solution)/shard_map/ppermute | solution.py:210
  10.6 0.0 collective-permute-done
  10.6 0.0 copy-done.4
  10.6 0.7 %convolution_convert_fusion = bf16[512,1024]{0,1:T(8,128)(2,1)S(1)} fusion(bf16[1024,512]{1,0:T(8,128)(2,1)S(1)} %bitcast.20, bf16[512,512]{1,0:T(8,128)(2,1)S(1)} %copy-done.4), kind=kOutput, calls=%fused_computation | convolution fusion | flops 537395200 | bytes 2621440 | tf_op jit(solution)/shard_map/dot_general | solution.py:216
  11.3 0.1 collective-permute-done.3.refs_3_
  11.5 0.0 copy-done
  11.5 0.0 copy-done.1
  11.5 0.0 copy-done.2
  11.5 0.0 copy-done.3
  11.5 19.6 %shard_map.91 = bf16[8,9,128,512]{3,2,1,0:T(8,128)(2,1)} custom-call(s32[1]{0:T(128)} %bitcast.block, s32[16]{0:T(128)S(1)} %copy-done.3, s32[16,9]{1,0:T(8,128)S(1)} %copy-done, s32[8,9]{1,0:T(8,128)S(1)} %copy-done.1, s32[8,9]{1,0:T(8,128)S(1)} %copy-done.2, bf16[8,128,512]{2,1,0:T(8,128)(2,1)S(1)} %bitcast.17, bf16[8,128,512]{2,1,0:T(8,128)(2,1)S(1)} %bitcast.18, ...), custom_call_target="tpu_custom_call" | custom-call | flops 9663676416 | bytes 9437184 | tf_op jit(solution)/shard_map/pallas_call | solution.py:174
  (7 shorter events, 0.0 us)
Async XLA Ops:
  0.0 10.6 %copy-start.4 = (bf16[512,512]{1,0:T(8,128)(2,1)S(1)}, bf16[512,512]{1,0:T(8,128)(2,1)}, u32[]{:S(2)}) copy-start(bf16[512,512]{1,0:T(8,128)(2,1)} %constant.31.clone.refs_4_) | copy-start | bytes 1572868
  0.0 10.6 %collective-permute-start = (bf16[8,128,512]{2,1,0:T(8,128)(2,1)}, bf16[8,128,512]{2,1,0:T(8,128)(2,1)S(1)}, u32[]{:S(2)}, u32[]{:S(2)}) collective-permute-start(bf16[8,128,512]{2,1,0:T(8,128)(2,1)} %param.9), channel_id=1, source_target_pairs={{16,0},{0,16},{17,1},{1,17},{18,2},{2,18},{19,3},{3,19},{20,4},{4,... | collective-permute-start | bytes 3145736 | tf_op jit(solution)/shard_map/ppermute | solution.py:210
  1.6 6.4 %collective-permute-start.1 = (bf16[8,512]{1,0:T(8,128)(2,1)S(1)}, bf16[8,512]{1,0:T(8,128)(2,1)S(1)}, u32[]{:S(2)}, u32[]{:S(2)}) collective-permute-start(bf16[8,512]{1,0:T(8,128)(2,1)S(1)} %get-tuple-element.7), channel_id=1, source_target_pairs={{0,1},{1,0},{2,3},{3,2},{4,5},{5,4},{6,7},{7,6},{8,9},{9,8},{10,11... | collective-permute-start | bytes 24584 | tf_op jit(solution)/shard_map/ppermute | solution.py:198
  2.9 6.2 %collective-permute-start.2 = (bf16[8,512]{1,0:T(8,128)(2,1)S(1)}, bf16[8,512]{1,0:T(8,128)(2,1)S(1)}, u32[]{:S(2)}, u32[]{:S(2)}) collective-permute-start(bf16[8,512]{1,0:T(8,128)(2,1)S(1)} %get-tuple-element.8), channel_id=1, source_target_pairs={{1,2},{3,4},{5,6},{7,8},{9,10},{11,12},{13,14},{2,1},{4,3},{6,5},{... | collective-permute-start | bytes 24584 | tf_op jit(solution)/shard_map/ppermute | solution.py:199
  7.9 3.5 %copy-start = (s32[16,9]{1,0:T(8,128)S(1)}, s32[16,9]{1,0:T(8,128)}, u32[]{:S(2)}) copy-start(s32[16,9]{1,0:T(8,128)} %partner.1) | copy-start | bytes 1732
  8.0 3.5 %copy-start.1 = (s32[8,9]{1,0:T(8,128)S(1)}, s32[8,9]{1,0:T(8,128)}, u32[]{:S(2)}) copy-start(s32[8,9]{1,0:T(8,128)} %low.1) | copy-start | bytes 868
  8.0 3.5 %copy-start.2 = (s32[8,9]{1,0:T(8,128)S(1)}, s32[8,9]{1,0:T(8,128)}, u32[]{:S(2)}) copy-start(s32[8,9]{1,0:T(8,128)} %high.1) | copy-start | bytes 868
  8.0 3.5 %copy-start.3 = (s32[16]{0:T(128)S(1)}, s32[16]{0:T(128)}, u32[]{:S(2)}) copy-start(s32[16]{0:T(128)} %count.1) | copy-start | bytes 196
  8.0 3.5 %copy-start.5 = (bf16[256,256]{1,0:T(8,128)(2,1)S(1)}, bf16[256,256]{1,0:T(8,128)(2,1)}, u32[]{:S(2)}) copy-start(bf16[256,256]{1,0:T(8,128)(2,1)} %constant.34.clone.refs_7_) | copy-start | bytes 393220
  8.0 3.5 %copy-start.6 = (bf16[256,256]{1,0:T(8,128)(2,1)S(1)}, bf16[256,256]{1,0:T(8,128)(2,1)}, u32[]{:S(2)}) copy-start(bf16[256,256]{1,0:T(8,128)(2,1)} %constant.33.clone.refs_6_) | copy-start | bytes 393220
  8.0 3.5 %copy-start.7 = (bf16[256,256]{1,0:T(8,128)(2,1)S(1)}, bf16[256,256]{1,0:T(8,128)(2,1)}, u32[]{:S(2)}) copy-start(bf16[256,256]{1,0:T(8,128)(2,1)} %constant.32.clone.refs_5_) | copy-start | bytes 393220
  9.1 2.4 %collective-permute-start.3 = (bf16[16,512]{1,0:T(8,128)(2,1)S(1)}, bf16[16,512]{1,0:T(8,128)(2,1)S(1)}, u32[]{:S(2)}, u32[]{:S(2)}) collective-permute-start(bf16[16,512]{1,0:T(8,128)(2,1)S(1)} %pad_maximum_fusion.refs_2_), channel_id=1, source_target_pairs={{16,0},{0,16},{17,1},{1,17},{18,2},{2,18},{19,3},{3,19},{20,4},{4,... | collective-permute-start | bytes 49160 | tf_op jit(solution)/shard_map/ppermute | solution.py:210

commit v5 on v4

--- a/solution.py
+++ b/solution.py
@@ -197,8 +197,7 @@
     outer = [(i, i + 1) for i in range(1, n - 1, 2)] + [(i + 1, i) for i in range(1, n - 1, 2)]
     from_inner = lax.ppermute(jnp.where(even, last, first), "space", inner)
     from_outer = lax.ppermute(jnp.where(even, first, last), "space", outer)
-    odd = jnp.logical_not(even)
-    return jnp.concatenate([jnp.where(odd, from_inner, from_outer), jnp.where(odd, from_outer, from_inner)], 0)
+    return jnp.concatenate([jnp.where(even, from_outer, from_inner), jnp.where(even, from_inner, from_outer)], 0)
 
 
 def local(acquisitions, partner, pair_count, band_low, band_high):

time: 31.3 us -> 30.7 us (0.981)
  the two profiles are of different devices: /device:TPU:25 before, /device:TPU:0 now
where the time goes in v5:
time: 30.7 us; the launch traced here: 30.5 us
  Pallas kernels  19.6 us (64%)
  starting transfers between devices  6.54 us (21%)
  matrix products  2.75 us (9%)
  local copies, waits for them, and re-layouts  0.95 us (3%)
  waiting for transfers between devices  0.45 us (1%)
    pallas_call x1, Pallas kernels, pairs(): pl.pallas_call(functools.partial(pairs_kernel, blocks=blocks), in_specs=[...  19.6 us
    ppermute x1, starting transfers between devices, edge_rows(): from_inner = lax.ppermute(jnp.where(even, last, first), 'space', inner)  5.35 us
    dot_general x2, matrix products, local(): spectrum = jnp.dot(strip, tables[0], preferred_element_type=F32).astype(BF)  2.75 us
    slice x1, local copies, waits for them, and re-layouts, edge_rows(): first, last = (strips[:, 0, :], strips[:, -1, :])  0.9 us
    ppermute x1, starting transfers between devices, edge_rows(): from_outer = lax.ppermute(jnp.where(even, first, last), 'space', outer)  0.66 us
  transfers between devices with their start and end apart: 4, of which 1 were waited for; matrix products, arithmetic and copies ran while one was open for 12% of the time, Pallas kernels for 0%

profile of v5, /device:TPU:0, one launch (start us, length us, event | category | flops | bytes accessed | tf_op | source)
XLA Modules:
  0.0 30.5 jit_solution(7273561379012793198)
XLA Ops:
  0.0 0.5 %collective-permute-start = (bf16[8,128,512]{2,1,0:T(8,128)(2,1)}, bf16[8,128,512]{2,1,0:T(8,128)(2,1)S(1)}, u32[]{:S(2)}, u32[]{:S(2)}) collective-permute-start(bf16[8,128,512]{2,1,0:T(8,128)(2,1)} %param.9), channel_id=1, source_target_pairs={{16,0},{0,16},{17,1},{1,17},{18,2},{2,18},{19,3},{3,19},{20,4},{4,... | collective-permute-start | bytes 3145736 | tf_op jit(solution)/shard_map/ppermute | solution.py:209
  0.5 0.9 %fusion = (bf16[8,1,512]{2,1,0:T(2,128)(2,1)S(1)}, bf16[8,1,512]{2,1,0:T(2,128)(2,1)S(1)}) fusion(bf16[8,128,512]{2,1,0:T(8,128)(2,1)} %param.9), kind=kLoop, calls=%fused_computation.7 | loop fusion | bytes 32768 | tf_op jit(solution)/shard_map/slice | solution.py:195
  1.4 0.7 %collective-permute-start.1 = (bf16[8,512]{1,0:T(8,128)(2,1)S(1)}, bf16[8,512]{1,0:T(8,128)(2,1)S(1)}, u32[]{:S(2)}, u32[]{:S(2)}) collective-permute-start(bf16[8,512]{1,0:T(8,128)(2,1)S(1)} %get-tuple-element.7), channel_id=1, source_target_pairs={{1,2},{3,4},{5,6},{7,8},{9,10},{11,12},{13,14},{2,1},{4,3},{6,5},{... | collective-permute-start | bytes 24584 | tf_op jit(solution)/shard_map/ppermute | solution.py:199
  2.0 5.3 %collective-permute-start.2 = (bf16[8,512]{1,0:T(8,128)(2,1)S(1)}, bf16[8,512]{1,0:T(8,128)(2,1)S(1)}, u32[]{:S(2)}, u32[]{:S(2)}) collective-permute-start(bf16[8,512]{1,0:T(8,128)(2,1)S(1)} %get-tuple-element.8), channel_id=1, source_target_pairs={{0,1},{1,0},{2,3},{3,2},{4,5},{5,4},{6,7},{7,6},{8,9},{9,8},{10,11... | collective-permute-start | bytes 24584 | tf_op jit(solution)/shard_map/ppermute | solution.py:198
  7.4 2.1 %convolution_convert_fusion.1 = bf16[512,1024]{0,1:T(8,128)(2,1)S(1)} fusion(bf16[1024,512]{1,0:T(8,128)(2,1)} %bitcast.19, bf16[512,512]{1,0:T(8,128)(2,1)} %constant.31.clone.refs_4_), kind=kOutput, calls=%fused_computation.1 | convolution fusion | flops 537395200 | bytes 2621440 | tf_op jit(solution)/shard_map/dot_general | solution.py:215
  9.5 0.0 copy-start
  9.5 0.0 copy-start.1
  9.5 0.0 copy-start.2
  9.5 0.0 copy-start.3
  9.5 0.0 copy-start.5
  9.5 0.0 copy-start.6
  9.5 0.0 copy-start.7
  9.5 0.0 collective-permute-done.1
  9.6 0.0 collective-permute-done.2
  9.6 0.1 collective-permute-start.3
  9.7 0.0 collective-permute-done
  9.7 0.0 copy-done.4
  9.7 0.7 %convolution_convert_fusion = bf16[512,1024]{0,1:T(8,128)(2,1)S(1)} fusion(bf16[1024,512]{1,0:T(8,128)(2,1)S(1)} %bitcast.20, bf16[512,512]{1,0:T(8,128)(2,1)S(1)} %copy-done.4), kind=kOutput, calls=%fused_computation | convolution fusion | flops 537395200 | bytes 2621440 | tf_op jit(solution)/shard_map/dot_general | solution.py:215
  10.4 0.4 %collective-permute-done.3.refs_3_ = bf16[16,512]{1,0:T(8,128)(2,1)S(1)} collective-permute-done((bf16[16,512]{1,0:T(8,128)(2,1)S(1)}, bf16[16,512]{1,0:T(8,128)(2,1)S(1)}, u32[]{:S(2)}, u32[]{:S(2)}) %collective-permute-start.3) | collective-permute-done | bytes 16416 | tf_op jit(solution)/shard_map/ppermute | solution.py:209
  10.9 0.0 copy-done.3
  10.9 0.0 copy-done.5
  10.9 0.0 copy-done.6
  10.9 0.0 copy-done.7
  10.9 19.6 %shard_map.91 = bf16[8,9,128,512]{3,2,1,0:T(8,128)(2,1)} custom-call(s32[1]{0:T(128)} %bitcast.block, s32[16]{0:T(128)S(1)} %copy-done.3, s32[16,9]{1,0:T(8,128)S(1)} %copy-done, s32[8,9]{1,0:T(8,128)S(1)} %copy-done.1, s32[8,9]{1,0:T(8,128)S(1)} %copy-done.2, bf16[8,128,512]{2,1,0:T(8,128)(2,1)S(1)} %bitcast.17, bf16[8,128,512]{2,1,0:T(8,128)(2,1)S(1)} %bitcast.18, ...), custom_call_target="tpu_custom_call" | custom-call | flops 9663676416 | bytes 9437184 | tf_op jit(solution)/shard_map/pallas_call | solution.py:174
  (7 shorter events, 0.0 us)
Async XLA Ops:
  0.0 9.7 %copy-start.4 = (bf16[512,512]{1,0:T(8,128)(2,1)S(1)}, bf16[512,512]{1,0:T(8,128)(2,1)}, u32[]{:S(2)}) copy-start(bf16[512,512]{1,0:T(8,128)(2,1)} %constant.31.clone.refs_4_) | copy-start | bytes 1572868
  0.0 9.7 %collective-permute-start = (bf16[8,128,512]{2,1,0:T(8,128)(2,1)}, bf16[8,128,512]{2,1,0:T(8,128)(2,1)S(1)}, u32[]{:S(2)}, u32[]{:S(2)}) collective-permute-start(bf16[8,128,512]{2,1,0:T(8,128)(2,1)} %param.9), channel_id=1, source_target_pairs={{16,0},{0,16},{17,1},{1,17},{18,2},{2,18},{19,3},{3,19},{20,4},{4,... | collective-permute-start | bytes 3145736 | tf_op jit(solution)/shard_map/ppermute | solution.py:209
  1.4 8.2 %collective-permute-start.1 = (bf16[8,512]{1,0:T(8,128)(2,1)S(1)}, bf16[8,512]{1,0:T(8,128)(2,1)S(1)}, u32[]{:S(2)}, u32[]{:S(2)}) collective-permute-start(bf16[8,512]{1,0:T(8,128)(2,1)S(1)} %get-tuple-element.7), channel_id=1, source_target_pairs={{1,2},{3,4},{5,6},{7,8},{9,10},{11,12},{13,14},{2,1},{4,3},{6,5},{... | collective-permute-start | bytes 24584 | tf_op jit(solution)/shard_map/ppermute | solution.py:199
  2.0 7.5 %collective-permute-start.2 = (bf16[8,512]{1,0:T(8,128)(2,1)S(1)}, bf16[8,512]{1,0:T(8,128)(2,1)S(1)}, u32[]{:S(2)}, u32[]{:S(2)}) collective-permute-start(bf16[8,512]{1,0:T(8,128)(2,1)S(1)} %get-tuple-element.8), channel_id=1, source_target_pairs={{0,1},{1,0},{2,3},{3,2},{4,5},{5,4},{6,7},{7,6},{8,9},{9,8},{10,11... | collective-permute-start | bytes 24584 | tf_op jit(solution)/shard_map/ppermute | solution.py:198
  9.5 1.4 %copy-start = (s32[16,9]{1,0:T(8,128)S(1)}, s32[16,9]{1,0:T(8,128)}, u32[]{:S(2)}) copy-start(s32[16,9]{1,0:T(8,128)} %partner.1) | copy-start | bytes 1732
  9.5 1.4 %copy-start.1 = (s32[8,9]{1,0:T(8,128)S(1)}, s32[8,9]{1,0:T(8,128)}, u32[]{:S(2)}) copy-start(s32[8,9]{1,0:T(8,128)} %low.1) | copy-start | bytes 868
  9.5 1.4 %copy-start.2 = (s32[8,9]{1,0:T(8,128)S(1)}, s32[8,9]{1,0:T(8,128)}, u32[]{:S(2)}) copy-start(s32[8,9]{1,0:T(8,128)} %high.1) | copy-start | bytes 868
  9.5 1.4 %copy-start.3 = (s32[16]{0:T(128)S(1)}, s32[16]{0:T(128)}, u32[]{:S(2)}) copy-start(s32[16]{0:T(128)} %count.1) | copy-start | bytes 196
  9.5 1.4 %copy-start.5 = (bf16[256,256]{1,0:T(8,128)(2,1)S(1)}, bf16[256,256]{1,0:T(8,128)(2,1)}, u32[]{:S(2)}) copy-start(bf16[256,256]{1,0:T(8,128)(2,1)} %constant.34.clone.refs_7_) | copy-start | bytes 393220
  9.5 1.4 %copy-start.6 = (bf16[256,256]{1,0:T(8,128)(2,1)S(1)}, bf16[256,256]{1,0:T(8,128)(2,1)}, u32[]{:S(2)}) copy-start(bf16[256,256]{1,0:T(8,128)(2,1)} %constant.33.clone.refs_6_) | copy-start | bytes 393220
  9.5 1.4 %copy-start.7 = (bf16[256,256]{1,0:T(8,128)(2,1)S(1)}, bf16[256,256]{1,0:T(8,128)(2,1)}, u32[]{:S(2)}) copy-start(bf16[256,256]{1,0:T(8,128)(2,1)} %constant.32.clone.refs_5_) | copy-start | bytes 393220
  9.6 1.2 %collective-permute-start.3 = (bf16[16,512]{1,0:T(8,128)(2,1)S(1)}, bf16[16,512]{1,0:T(8,128)(2,1)S(1)}, u32[]{:S(2)}, u32[]{:S(2)}) collective-permute-start(bf16[16,512]{1,0:T(8,128)(2,1)S(1)} %pad_maximum_fusion.refs_2_), channel_id=1, source_target_pairs={{16,0},{0,16},{17,1},{1,17},{18,2},{2,18},{19,3},{3,19},{20,4},{4,... | collective-permute-start | bytes 49160 | tf_op jit(solution)/shard_map/ppermute | solution.py:209

commit v6 on v5

--- a/solution.py
+++ b/solution.py
@@ -36,24 +36,15 @@
 
 
 def pairs_kernel(block, count, partner, low, high, *refs, blocks):
-    mains, edges, refs = refs[:blocks], refs[blocks : 2 * blocks], refs[2 * blocks :]
+    own, pool, edges, refs = refs[0], refs[1], refs[2 : 2 + blocks], refs[2 + blocks :]
     forward, inv_even, inv_odd, band, out = refs[:5]
-    spectra, sums, across, ready, main_sem, out_sem = refs[5:]
+    rims, sums, across, ready, out_sem = refs[5:]
     dates, slots = low.shape
-    ext, cols = spectra.shape[1:]
-    rows = ext - TILE
+    rows, cols = own.shape[1:]
+    ext = rows + TILE
     bins = cols // 2
     half = bins // 2
     here = block[0]
-
-    def main_copy(k, first, last, sem):
-        place = spectra.at[pl.ds(k * dates + first, last - first), pl.ds(0, rows)]
-        return pltpu.make_async_copy(mains[k].at[pl.ds(first, last - first)], place, main_sem.at[sem])
-
-    early = [main_copy(k, 0, dates, k) for k in range(1, blocks)] + [main_copy(0, 0, 1, 0)]
-    later = [main_copy(0, 1, dates, blocks)] if dates > 1 else []
-    for copy in early + later:
-        copy.start()
 
     tile_row = lax.broadcasted_iota(jnp.int32, (TILE, cols), 0)
     for k in range(blocks):
@@ -61,7 +52,7 @@
         for q in range(dates):
             before, after = edge[q : q + 1], edge[dates + q : dates + q + 1]
             tile = jnp.where(tile_row == 0, after, jnp.where(tile_row == TILE - 1, before, 0.0))
-            spectra[k * dates + q, rows:ext] = tile.astype(BF)
+            rims[k * dates + q] = tile.astype(BF)
 
     lane = lax.broadcasted_iota(jnp.int32, (TILE, cols), 1)
     bin_id = lane % half * 2 + lane // bins
@@ -76,9 +67,11 @@
         second = partner[whole_date, slot]
         away = second // dates - here
         away = jnp.where(away < 0, away + blocks, away)
-        tiled = (ext // TILE, TILE, cols)
-        a = (spectra[date].reshape(tiled) * mask).reshape(ext, cols)
-        b = (spectra[away * dates + second % dates].reshape(tiled) * mask).reshape(ext, cols)
+        other = jnp.maximum(away - 1, 0) * dates + second % dates
+        a = own[date].reshape(rows // TILE, TILE, cols) * mask
+        b = pool[other].reshape(rows // TILE, TILE, cols) * mask
+        a = jnp.concatenate([a.reshape(rows, cols), rims[date] * mask[0]], 0)
+        b = jnp.concatenate([b.reshape(rows, cols), rims[dates + other] * mask[0]], 0)
         return [a, b]
 
     def filter_date(date, ring, group):
@@ -123,15 +116,11 @@
     def send(date, ring):
         return pltpu.make_async_copy(ready.at[ring], out.at[date], out_sem.at[ring])
 
-    for copy in early:
-        copy.wait()
     parts_of_date = 1
     groups = [list(range(slots * g // parts_of_date, slots * (g + 1) // parts_of_date)) for g in range(parts_of_date)]
     groups = [g for g in groups if g]
     for group in groups:
         filter_date(0, 0, group)
-    for copy in later:
-        copy.wait()
 
     def body(date, _):
         now = lax.rem(date, 2)
@@ -170,23 +159,23 @@
     whole = pl.BlockSpec(memory_space=pltpu.VMEM)
     anywhere = pl.BlockSpec(memory_space=pl.ANY)
     blocks = len(mains)
+    pool = mains[1] if blocks == 2 else jnp.concatenate(mains[1:] or mains, 0)
     work = dates * slots * rows * cols
     return pl.pallas_call(
         functools.partial(pairs_kernel, blocks=blocks),
-        in_specs=[scalars] * 5 + [anywhere] * blocks + [whole] * (blocks + len(tables)),
+        in_specs=[scalars] * 5 + [whole] * (2 + blocks + len(tables)),
         out_specs=anywhere,
         out_shape=jax.ShapeDtypeStruct((dates, slots, rows, cols), BF),
         scratch_shapes=[
-            pltpu.VMEM((blocks * dates, ext, cols), BF),
+            pltpu.VMEM((blocks * dates, TILE, cols), BF),
             pltpu.VMEM((2, slots, 4 * ext, cols // 2), BF),
             pltpu.VMEM((slots, 8, ext, cols // 4), F32),
             pltpu.VMEM((2, slots, rows, cols), BF),
-            pltpu.SemaphoreType.DMA((blocks + 1,)),
             pltpu.SemaphoreType.DMA((2,)),
         ],
         cost_estimate=pl.CostEstimate(flops=work * cols * 4, bytes_accessed=work * 2, transcendentals=work // 2),
         compiler_params=pltpu.CompilerParams(vmem_limit_bytes=50 * 2**20),
-    )(block, count, partner, low, high, *mains, *edges, *tables)
+    )(block, count, partner, low, high, mains[0], pool, *edges, *tables)
 
 
 def edge_rows(strips):

time: 30.7 us -> 30.5 us (level)
  no operation moved by 1% of the time
where the time goes in v6:
time: 30.5 us; the launch traced here: 30.3 us
  Pallas kernels  19.4 us (64%)
  starting transfers between devices  6.54 us (21%)
  matrix products  2.75 us (9%)
  local copies, waits for them, and re-layouts  0.95 us (3%)
  waiting for transfers between devices  0.45 us (1%)
    pallas_call x1, Pallas kernels, pairs(): pl.pallas_call(functools.partial(pairs_kernel, blocks=blocks), in_specs=[...  19.4 us
    ppermute x1, starting transfers between devices, edge_rows(): from_inner = lax.ppermute(jnp.where(even, last, first), 'space', inner)  5.35 us
    dot_general x2, matrix products, local(): spectrum = jnp.dot(strip, tables[0], preferred_element_type=F32).astype(BF)  2.75 us
    slice x1, local copies, waits for them, and re-layouts, edge_rows(): first, last = (strips[:, 0, :], strips[:, -1, :])  0.9 us
    ppermute x1, starting transfers between devices, edge_rows(): from_outer = lax.ppermute(jnp.where(even, first, last), 'space', outer)  0.66 us
  transfers between devices with their start and end apart: 4, of which 1 were waited for; matrix products, arithmetic and copies ran while one was open for 12% of the time, Pallas kernels for 0%

profile of v6, /device:TPU:0, one launch (start us, length us, event | category | flops | bytes accessed | tf_op | source)
XLA Modules:
  0.0 30.3 jit_solution(16253366627917563652)
XLA Ops:
  0.0 0.5 %collective-permute-start = (bf16[8,128,512]{2,1,0:T(8,128)(2,1)}, bf16[8,128,512]{2,1,0:T(8,128)(2,1)S(1)}, u32[]{:S(2)}, u32[]{:S(2)}) collective-permute-start(bf16[8,128,512]{2,1,0:T(8,128)(2,1)} %param.9), channel_id=1, source_target_pairs={{16,0},{0,16},{17,1},{1,17},{18,2},{2,18},{19,3},{3,19},{20,4},{4,... | collective-permute-start | bytes 3145736 | tf_op jit(solution)/shard_map/ppermute | solution.py:198
  0.5 0.9 %fusion = (bf16[8,1,512]{2,1,0:T(2,128)(2,1)S(1)}, bf16[8,1,512]{2,1,0:T(2,128)(2,1)S(1)}) fusion(bf16[8,128,512]{2,1,0:T(8,128)(2,1)} %param.9), kind=kLoop, calls=%fused_computation.7 | loop fusion | bytes 32768 | tf_op jit(solution)/shard_map/slice | solution.py:184
  1.4 0.7 %collective-permute-start.1 = (bf16[8,512]{1,0:T(8,128)(2,1)S(1)}, bf16[8,512]{1,0:T(8,128)(2,1)S(1)}, u32[]{:S(2)}, u32[]{:S(2)}) collective-permute-start(bf16[8,512]{1,0:T(8,128)(2,1)S(1)} %get-tuple-element.7), channel_id=1, source_target_pairs={{1,2},{3,4},{5,6},{7,8},{9,10},{11,12},{13,14},{2,1},{4,3},{6,5},{... | collective-permute-start | bytes 24584 | tf_op jit(solution)/shard_map/ppermute | solution.py:188
  2.0 5.3 %collective-permute-start.2 = (bf16[8,512]{1,0:T(8,128)(2,1)S(1)}, bf16[8,512]{1,0:T(8,128)(2,1)S(1)}, u32[]{:S(2)}, u32[]{:S(2)}) collective-permute-start(bf16[8,512]{1,0:T(8,128)(2,1)S(1)} %get-tuple-element.8), channel_id=1, source_target_pairs={{0,1},{1,0},{2,3},{3,2},{4,5},{5,4},{6,7},{7,6},{8,9},{9,8},{10,11... | collective-permute-start | bytes 24584 | tf_op jit(solution)/shard_map/ppermute | solution.py:187
  7.4 2.1 %convolution_convert_fusion.1 = bf16[512,1024]{0,1:T(8,128)(2,1)S(1)} fusion(bf16[1024,512]{1,0:T(8,128)(2,1)} %bitcast.19, bf16[512,512]{1,0:T(8,128)(2,1)} %constant.31.clone.refs_4_), kind=kOutput, calls=%fused_computation.1 | convolution fusion | flops 537395200 | bytes 2621440 | tf_op jit(solution)/shard_map/dot_general | solution.py:204
  9.5 0.0 copy-start
  9.5 0.0 copy-start.1
  9.5 0.0 copy-start.2
  9.5 0.0 copy-start.3
  9.5 0.0 copy-start.5
  9.5 0.0 copy-start.6
  9.5 0.0 copy-start.7
  9.5 0.0 collective-permute-done.1
  9.6 0.0 collective-permute-done.2
  9.6 0.1 collective-permute-start.3
  9.7 0.0 collective-permute-done
  9.7 0.0 copy-done.4
  9.7 0.7 %convolution_convert_fusion = bf16[512,1024]{0,1:T(8,128)(2,1)S(1)} fusion(bf16[1024,512]{1,0:T(8,128)(2,1)S(1)} %bitcast.20, bf16[512,512]{1,0:T(8,128)(2,1)S(1)} %copy-done.4), kind=kOutput, calls=%fused_computation | convolution fusion | flops 537395200 | bytes 2621440 | tf_op jit(solution)/shard_map/dot_general | solution.py:204
  10.4 0.4 %collective-permute-done.3.refs_3_ = bf16[16,512]{1,0:T(8,128)(2,1)S(1)} collective-permute-done((bf16[16,512]{1,0:T(8,128)(2,1)S(1)}, bf16[16,512]{1,0:T(8,128)(2,1)S(1)}, u32[]{:S(2)}, u32[]{:S(2)}) %collective-permute-start.3) | collective-permute-done | bytes 16416 | tf_op jit(solution)/shard_map/ppermute | solution.py:198
  10.8 0.0 copy-done
  10.8 0.0 copy-done.1
  10.9 0.0 copy-done.2
  10.9 0.0 copy-done.3
  10.9 19.4 %shard_map.91 = bf16[8,9,128,512]{3,2,1,0:T(8,128)(2,1)} custom-call(s32[1]{0:T(128)} %bitcast.block, s32[16]{0:T(128)S(1)} %copy-done.3, s32[16,9]{1,0:T(8,128)S(1)} %copy-done, s32[8,9]{1,0:T(8,128)S(1)} %copy-done.1, s32[8,9]{1,0:T(8,128)S(1)} %copy-done.2, bf16[8,128,512]{2,1,0:T(8,128)(2,1)S(1)} %bitcast.17, bf16[8,128,512]{2,1,0:T(8,128)(2,1)S(1)} %bitcast.18, ...), custom_call_target="tpu_custom_call" | custom-call | flops 9663676416 | bytes 9437184 | tf_op jit(solution)/shard_map/pallas_call | solution.py:164
  (7 shorter events, 0.0 us)
Async XLA Ops:
  0.0 9.7 %copy-start.4 = (bf16[512,512]{1,0:T(8,128)(2,1)S(1)}, bf16[512,512]{1,0:T(8,128)(2,1)}, u32[]{:S(2)}) copy-start(bf16[512,512]{1,0:T(8,128)(2,1)} %constant.31.clone.refs_4_) | copy-start | bytes 1572868
  0.0 9.7 %collective-permute-start = (bf16[8,128,512]{2,1,0:T(8,128)(2,1)}, bf16[8,128,512]{2,1,0:T(8,128)(2,1)S(1)}, u32[]{:S(2)}, u32[]{:S(2)}) collective-permute-start(bf16[8,128,512]{2,1,0:T(8,128)(2,1)} %param.9), channel_id=1, source_target_pairs={{16,0},{0,16},{17,1},{1,17},{18,2},{2,18},{19,3},{3,19},{20,4},{4,... | collective-permute-start | bytes 3145736 | tf_op jit(solution)/shard_map/ppermute | solution.py:198
  1.4 8.2 %collective-permute-start.1 = (bf16[8,512]{1,0:T(8,128)(2,1)S(1)}, bf16[8,512]{1,0:T(8,128)(2,1)S(1)}, u32[]{:S(2)}, u32[]{:S(2)}) collective-permute-start(bf16[8,512]{1,0:T(8,128)(2,1)S(1)} %get-tuple-element.7), channel_id=1, source_target_pairs={{1,2},{3,4},{5,6},{7,8},{9,10},{11,12},{13,14},{2,1},{4,3},{6,5},{... | collective-permute-start | bytes 24584 | tf_op jit(solution)/shard_map/ppermute | solution.py:188
  2.0 7.5 %collective-permute-start.2 = (bf16[8,512]{1,0:T(8,128)(2,1)S(1)}, bf16[8,512]{1,0:T(8,128)(2,1)S(1)}, u32[]{:S(2)}, u32[]{:S(2)}) collective-permute-start(bf16[8,512]{1,0:T(8,128)(2,1)S(1)} %get-tuple-element.8), channel_id=1, source_target_pairs={{0,1},{1,0},{2,3},{3,2},{4,5},{5,4},{6,7},{7,6},{8,9},{9,8},{10,11... | collective-permute-start | bytes 24584 | tf_op jit(solution)/shard_map/ppermute | solution.py:187
  9.5 1.4 %copy-start = (s32[16,9]{1,0:T(8,128)S(1)}, s32[16,9]{1,0:T(8,128)}, u32[]{:S(2)}) copy-start(s32[16,9]{1,0:T(8,128)} %partner.1) | copy-start | bytes 1732
  9.5 1.4 %copy-start.1 = (s32[8,9]{1,0:T(8,128)S(1)}, s32[8,9]{1,0:T(8,128)}, u32[]{:S(2)}) copy-start(s32[8,9]{1,0:T(8,128)} %low.1) | copy-start | bytes 868
  9.5 1.4 %copy-start.2 = (s32[8,9]{1,0:T(8,128)S(1)}, s32[8,9]{1,0:T(8,128)}, u32[]{:S(2)}) copy-start(s32[8,9]{1,0:T(8,128)} %high.1) | copy-start | bytes 868
  9.5 1.4 %copy-start.3 = (s32[16]{0:T(128)S(1)}, s32[16]{0:T(128)}, u32[]{:S(2)}) copy-start(s32[16]{0:T(128)} %count.1) | copy-start | bytes 196
  9.5 1.4 %copy-start.5 = (bf16[256,256]{1,0:T(8,128)(2,1)S(1)}, bf16[256,256]{1,0:T(8,128)(2,1)}, u32[]{:S(2)}) copy-start(bf16[256,256]{1,0:T(8,128)(2,1)} %constant.34.clone.refs_7_) | copy-start | bytes 393220
  9.5 1.4 %copy-start.6 = (bf16[256,256]{1,0:T(8,128)(2,1)S(1)}, bf16[256,256]{1,0:T(8,128)(2,1)}, u32[]{:S(2)}) copy-start(bf16[256,256]{1,0:T(8,128)(2,1)} %constant.33.clone.refs_6_) | copy-start | bytes 393220
  9.5 1.4 %copy-start.7 = (bf16[256,256]{1,0:T(8,128)(2,1)S(1)}, bf16[256,256]{1,0:T(8,128)(2,1)}, u32[]{:S(2)}) copy-start(bf16[256,256]{1,0:T(8,128)(2,1)} %constant.32.clone.refs_5_) | copy-start | bytes 393220
  9.6 1.2 %collective-permute-start.3 = (bf16[16,512]{1,0:T(8,128)(2,1)S(1)}, bf16[16,512]{1,0:T(8,128)(2,1)S(1)}, u32[]{:S(2)}, u32[]{:S(2)}) collective-permute-start(bf16[16,512]{1,0:T(8,128)(2,1)S(1)} %pad_maximum_fusion.refs_2_), channel_id=1, source_target_pairs={{16,0},{0,16},{17,1},{1,17},{18,2},{2,18},{19,3},{3,19},{20,4},{4,... | collective-permute-start | bytes 49160 | tf_op jit(solution)/shard_map/ppermute | solution.py:198

commit v7 on v6

--- a/solution.py
+++ b/solution.py
@@ -47,8 +47,9 @@
     here = block[0]
 
     tile_row = lax.broadcasted_iota(jnp.int32, (TILE, cols), 0)
+    edge_spectra = dot(jnp.concatenate([edge[...] for edge in edges], 0), forward[...]).astype(BF).astype(F32)
     for k in range(blocks):
-        edge = dot(edges[k][...], forward[...]).astype(BF).astype(F32)
+        edge = edge_spectra[2 * dates * k : 2 * dates * (k + 1)]
         for q in range(dates):
             before, after = edge[q : q + 1], edge[dates + q : dates + q + 1]
             tile = jnp.where(tile_row == 0, after, jnp.where(tile_row == TILE - 1, before, 0.0))
@@ -95,7 +96,11 @@
         flat = jnp.concatenate([sums[ring, slot] for slot in group], 0)
         cut = flat.shape[0] // (2 * TILE) * TILE
         summed = jnp.concatenate([dot(flat[:cut], window), dot(flat[cut:], window)], 0)
-        for i, slot in enumerate(group):
+        middle = (len(group) + 1) // 2
+        turns = [i for pair in zip(range(middle), range(middle, len(group))) for i in pair]
+        turns += list(range(len(group) // 2, middle))
+        for i in turns:
+            slot = group[i]
             looked = []
             for q in range(4):
                 parts = []

time: 30.5 us -> 30.4 us (level)
  no operation moved by 1% of the time
where the time goes in v7:
time: 30.4 us; the launch traced here: 30.2 us
  Pallas kernels  19.3 us (63%)
  starting transfers between devices  6.54 us (22%)
  matrix products  2.75 us (9%)
  local copies, waits for them, and re-layouts  0.95 us (3%)
  waiting for transfers between devices  0.45 us (1%)
    pallas_call x1, Pallas kernels, pairs(): pl.pallas_call(functools.partial(pairs_kernel, blocks=blocks), in_specs=[...  19.3 us
    ppermute x1, starting transfers between devices, edge_rows(): from_inner = lax.ppermute(jnp.where(even, last, first), 'space', inner)  5.35 us
    dot_general x2, matrix products, local(): spectrum = jnp.dot(strip, tables[0], preferred_element_type=F32).astype(BF)  2.75 us
    slice x1, local copies, waits for them, and re-layouts, edge_rows(): first, last = (strips[:, 0, :], strips[:, -1, :])  0.9 us
    ppermute x1, starting transfers between devices, edge_rows(): from_outer = lax.ppermute(jnp.where(even, first, last), 'space', outer)  0.66 us
  transfers between devices with their start and end apart: 4, of which 1 were waited for; matrix products, arithmetic and copies ran while one was open for 12% of the time, Pallas kernels for 0%

profile of v7, /device:TPU:0, one launch (start us, length us, event | category | flops | bytes accessed | tf_op | source)
XLA Modules:
  0.0 30.2 jit_solution(4919765443268580458)
XLA Ops:
  0.0 0.5 %collective-permute-start = (bf16[8,128,512]{2,1,0:T(8,128)(2,1)}, bf16[8,128,512]{2,1,0:T(8,128)(2,1)S(1)}, u32[]{:S(2)}, u32[]{:S(2)}) collective-permute-start(bf16[8,128,512]{2,1,0:T(8,128)(2,1)} %param.9), channel_id=1, source_target_pairs={{16,0},{0,16},{17,1},{1,17},{18,2},{2,18},{19,3},{3,19},{20,4},{4,... | collective-permute-start | bytes 3145736 | tf_op jit(solution)/shard_map/ppermute | solution.py:203
  0.5 0.9 %fusion = (bf16[8,1,512]{2,1,0:T(2,128)(2,1)S(1)}, bf16[8,1,512]{2,1,0:T(2,128)(2,1)S(1)}) fusion(bf16[8,128,512]{2,1,0:T(8,128)(2,1)} %param.9), kind=kLoop, calls=%fused_computation.7 | loop fusion | bytes 32768 | tf_op jit(solution)/shard_map/slice | solution.py:189
  1.4 0.7 %collective-permute-start.1 = (bf16[8,512]{1,0:T(8,128)(2,1)S(1)}, bf16[8,512]{1,0:T(8,128)(2,1)S(1)}, u32[]{:S(2)}, u32[]{:S(2)}) collective-permute-start(bf16[8,512]{1,0:T(8,128)(2,1)S(1)} %get-tuple-element.7), channel_id=1, source_target_pairs={{1,2},{3,4},{5,6},{7,8},{9,10},{11,12},{13,14},{2,1},{4,3},{6,5},{... | collective-permute-start | bytes 24584 | tf_op jit(solution)/shard_map/ppermute | solution.py:193
  2.0 5.3 %collective-permute-start.2 = (bf16[8,512]{1,0:T(8,128)(2,1)S(1)}, bf16[8,512]{1,0:T(8,128)(2,1)S(1)}, u32[]{:S(2)}, u32[]{:S(2)}) collective-permute-start(bf16[8,512]{1,0:T(8,128)(2,1)S(1)} %get-tuple-element.8), channel_id=1, source_target_pairs={{0,1},{1,0},{2,3},{3,2},{4,5},{5,4},{6,7},{7,6},{8,9},{9,8},{10,11... | collective-permute-start | bytes 24584 | tf_op jit(solution)/shard_map/ppermute | solution.py:192
  7.4 2.1 %convolution_convert_fusion.1 = bf16[512,1024]{0,1:T(8,128)(2,1)S(1)} fusion(bf16[1024,512]{1,0:T(8,128)(2,1)} %bitcast.19, bf16[512,512]{1,0:T(8,128)(2,1)} %constant.31.clone.refs_4_), kind=kOutput, calls=%fused_computation.1 | convolution fusion | flops 537395200 | bytes 2621440 | tf_op jit(solution)/shard_map/dot_general | solution.py:209
  9.5 0.0 copy-start
  9.5 0.0 copy-start.1
  9.5 0.0 copy-start.2
  9.5 0.0 copy-start.3
  9.5 0.0 copy-start.5
  9.5 0.0 copy-start.6
  9.5 0.0 copy-start.7
  9.5 0.0 collective-permute-done.1
  9.6 0.0 collective-permute-done.2
  9.6 0.1 collective-permute-start.3
  9.7 0.0 collective-permute-done
  9.7 0.0 copy-done.4
  9.7 0.7 %convolution_convert_fusion = bf16[512,1024]{0,1:T(8,128)(2,1)S(1)} fusion(bf16[1024,512]{1,0:T(8,128)(2,1)S(1)} %bitcast.20, bf16[512,512]{1,0:T(8,128)(2,1)S(1)} %copy-done.4), kind=kOutput, calls=%fused_computation | convolution fusion | flops 537395200 | bytes 2621440 | tf_op jit(solution)/shard_map/dot_general | solution.py:209
  10.4 0.4 %collective-permute-done.3.refs_3_ = bf16[16,512]{1,0:T(8,128)(2,1)S(1)} collective-permute-done((bf16[16,512]{1,0:T(8,128)(2,1)S(1)}, bf16[16,512]{1,0:T(8,128)(2,1)S(1)}, u32[]{:S(2)}, u32[]{:S(2)}) %collective-permute-start.3) | collective-permute-done | bytes 16416 | tf_op jit(solution)/shard_map/ppermute | solution.py:203
  10.8 0.0 copy-done
  10.8 0.0 copy-done.1
  10.9 0.0 copy-done.2
  10.9 0.0 copy-done.3
  10.9 19.3 %shard_map.91 = bf16[8,9,128,512]{3,2,1,0:T(8,128)(2,1)} custom-call(s32[1]{0:T(128)} %bitcast.block, s32[16]{0:T(128)S(1)} %copy-done.3, s32[16,9]{1,0:T(8,128)S(1)} %copy-done, s32[8,9]{1,0:T(8,128)S(1)} %copy-done.1, s32[8,9]{1,0:T(8,128)S(1)} %copy-done.2, bf16[8,128,512]{2,1,0:T(8,128)(2,1)S(1)} %bitcast.17, bf16[8,128,512]{2,1,0:T(8,128)(2,1)S(1)} %bitcast.18, ...), custom_call_target="tpu_custom_call" | custom-call | flops 9663676416 | bytes 9437184 | tf_op jit(solution)/shard_map/pallas_call | solution.py:169
  (7 shorter events, 0.0 us)
Async XLA Ops:
  0.0 9.7 %copy-start.4 = (bf16[512,512]{1,0:T(8,128)(2,1)S(1)}, bf16[512,512]{1,0:T(8,128)(2,1)}, u32[]{:S(2)}) copy-start(bf16[512,512]{1,0:T(8,128)(2,1)} %constant.31.clone.refs_4_) | copy-start | bytes 1572868
  0.0 9.7 %collective-permute-start = (bf16[8,128,512]{2,1,0:T(8,128)(2,1)}, bf16[8,128,512]{2,1,0:T(8,128)(2,1)S(1)}, u32[]{:S(2)}, u32[]{:S(2)}) collective-permute-start(bf16[8,128,512]{2,1,0:T(8,128)(2,1)} %param.9), channel_id=1, source_target_pairs={{16,0},{0,16},{17,1},{1,17},{18,2},{2,18},{19,3},{3,19},{20,4},{4,... | collective-permute-start | bytes 3145736 | tf_op jit(solution)/shard_map/ppermute | solution.py:203
  1.4 8.2 %collective-permute-start.1 = (bf16[8,512]{1,0:T(8,128)(2,1)S(1)}, bf16[8,512]{1,0:T(8,128)(2,1)S(1)}, u32[]{:S(2)}, u32[]{:S(2)}) collective-permute-start(bf16[8,512]{1,0:T(8,128)(2,1)S(1)} %get-tuple-element.7), channel_id=1, source_target_pairs={{1,2},{3,4},{5,6},{7,8},{9,10},{11,12},{13,14},{2,1},{4,3},{6,5},{... | collective-permute-start | bytes 24584 | tf_op jit(solution)/shard_map/ppermute | solution.py:193
  2.0 7.5 %collective-permute-start.2 = (bf16[8,512]{1,0:T(8,128)(2,1)S(1)}, bf16[8,512]{1,0:T(8,128)(2,1)S(1)}, u32[]{:S(2)}, u32[]{:S(2)}) collective-permute-start(bf16[8,512]{1,0:T(8,128)(2,1)S(1)} %get-tuple-element.8), channel_id=1, source_target_pairs={{0,1},{1,0},{2,3},{3,2},{4,5},{5,4},{6,7},{7,6},{8,9},{9,8},{10,11... | collective-permute-start | bytes 24584 | tf_op jit(solution)/shard_map/ppermute | solution.py:192
  9.5 1.4 %copy-start = (s32[16,9]{1,0:T(8,128)S(1)}, s32[16,9]{1,0:T(8,128)}, u32[]{:S(2)}) copy-start(s32[16,9]{1,0:T(8,128)} %partner.1) | copy-start | bytes 1732
  9.5 1.4 %copy-start.1 = (s32[8,9]{1,0:T(8,128)S(1)}, s32[8,9]{1,0:T(8,128)}, u32[]{:S(2)}) copy-start(s32[8,9]{1,0:T(8,128)} %low.1) | copy-start | bytes 868
  9.5 1.4 %copy-start.2 = (s32[8,9]{1,0:T(8,128)S(1)}, s32[8,9]{1,0:T(8,128)}, u32[]{:S(2)}) copy-start(s32[8,9]{1,0:T(8,128)} %high.1) | copy-start | bytes 868
  9.5 1.4 %copy-start.3 = (s32[16]{0:T(128)S(1)}, s32[16]{0:T(128)}, u32[]{:S(2)}) copy-start(s32[16]{0:T(128)} %count.1) | copy-start | bytes 196
  9.5 1.4 %copy-start.5 = (bf16[256,256]{1,0:T(8,128)(2,1)S(1)}, bf16[256,256]{1,0:T(8,128)(2,1)}, u32[]{:S(2)}) copy-start(bf16[256,256]{1,0:T(8,128)(2,1)} %constant.34.clone.refs_7_) | copy-start | bytes 393220
  9.5 1.4 %copy-start.6 = (bf16[256,256]{1,0:T(8,128)(2,1)S(1)}, bf16[256,256]{1,0:T(8,128)(2,1)}, u32[]{:S(2)}) copy-start(bf16[256,256]{1,0:T(8,128)(2,1)} %constant.33.clone.refs_6_) | copy-start | bytes 393220
  9.5 1.4 %copy-start.7 = (bf16[256,256]{1,0:T(8,128)(2,1)S(1)}, bf16[256,256]{1,0:T(8,128)(2,1)}, u32[]{:S(2)}) copy-start(bf16[256,256]{1,0:T(8,128)(2,1)} %constant.32.clone.refs_5_) | copy-start | bytes 393220
  9.6 1.2 %collective-permute-start.3 = (bf16[16,512]{1,0:T(8,128)(2,1)S(1)}, bf16[16,512]{1,0:T(8,128)(2,1)S(1)}, u32[]{:S(2)}, u32[]{:S(2)}) collective-permute-start(bf16[16,512]{1,0:T(8,128)(2,1)S(1)} %pad_maximum_fusion.refs_2_), channel_id=1, source_target_pairs={{16,0},{0,16},{17,1},{1,17},{18,2},{2,18},{19,3},{3,19},{20,4},{4,... | collective-permute-start | bytes 49160 | tf_op jit(solution)/shard_map/ppermute | solution.py:203

commit v8 on v7

--- a/solution.py
+++ b/solution.py
@@ -109,7 +109,7 @@
                     held = across.at[slot, 2 * q + c]
                     held[0:SUB] = v[ext - SUB :]
                     held[SUB:ext] = v[: ext - SUB]
-                    up = pltpu.roll(v, 1, 0)[:rows] if q < 2 else held[SUB - 1 : SUB - 1 + rows]
+                    up = pltpu.roll(v, 1, 0)[:rows] if q >= 2 else held[SUB - 1 : SUB - 1 + rows]
                     parts.append(up + v[:rows] + held[SUB + 1 : SUB + 1 + rows])
                 looked.append(jnp.concatenate(parts, 1))
             scale = lax.rsqrt(jnp.maximum(looked[2], 1.0) * jnp.maximum(looked[3], 1.0))

time: 30.4 us -> 30.2 us (level)
  no operation moved by 1% of the time
where the time goes in v8:
time: 30.2 us; the launch traced here: 30.1 us
  Pallas kernels  19.2 us (64%)
  starting transfers between devices  6.54 us (22%)
  matrix products  2.75 us (9%)
  local copies, waits for them, and re-layouts  0.95 us (3%)
  waiting for transfers between devices  0.45 us (1%)
    pallas_call x1, Pallas kernels, pairs(): pl.pallas_call(functools.partial(pairs_kernel, blocks=blocks), in_specs=[...  19.2 us
    ppermute x1, starting transfers between devices, edge_rows(): from_inner = lax.ppermute(jnp.where(even, last, first), 'space', inner)  5.35 us
    dot_general x2, matrix products, local(): spectrum = jnp.dot(strip, tables[0], preferred_element_type=F32).astype(BF)  2.75 us
    slice x1, local copies, waits for them, and re-layouts, edge_rows(): first, last = (strips[:, 0, :], strips[:, -1, :])  0.9 us
    ppermute x1, starting transfers between devices, edge_rows(): from_outer = lax.ppermute(jnp.where(even, first, last), 'space', outer)  0.66 us
  transfers between devices with their start and end apart: 4, of which 1 were waited for; matrix products, arithmetic and copies ran while one was open for 12% of the time, Pallas kernels for 0%

profile of v8, /device:TPU:0, one launch (start us, length us, event | category | flops | bytes accessed | tf_op | source)
XLA Modules:
  0.0 30.1 jit_solution(13999837589658450335)
XLA Ops:
  0.0 0.5 %collective-permute-start = (bf16[8,128,512]{2,1,0:T(8,128)(2,1)}, bf16[8,128,512]{2,1,0:T(8,128)(2,1)S(1)}, u32[]{:S(2)}, u32[]{:S(2)}) collective-permute-start(bf16[8,128,512]{2,1,0:T(8,128)(2,1)} %param.9), channel_id=1, source_target_pairs={{16,0},{0,16},{17,1},{1,17},{18,2},{2,18},{19,3},{3,19},{20,4},{4,... | collective-permute-start | bytes 3145736 | tf_op jit(solution)/shard_map/ppermute | solution.py:203
  0.5 0.9 %fusion = (bf16[8,1,512]{2,1,0:T(2,128)(2,1)S(1)}, bf16[8,1,512]{2,1,0:T(2,128)(2,1)S(1)}) fusion(bf16[8,128,512]{2,1,0:T(8,128)(2,1)} %param.9), kind=kLoop, calls=%fused_computation.7 | loop fusion | bytes 32768 | tf_op jit(solution)/shard_map/slice | solution.py:189
  1.4 0.7 %collective-permute-start.1 = (bf16[8,512]{1,0:T(8,128)(2,1)S(1)}, bf16[8,512]{1,0:T(8,128)(2,1)S(1)}, u32[]{:S(2)}, u32[]{:S(2)}) collective-permute-start(bf16[8,512]{1,0:T(8,128)(2,1)S(1)} %get-tuple-element.7), channel_id=1, source_target_pairs={{1,2},{3,4},{5,6},{7,8},{9,10},{11,12},{13,14},{2,1},{4,3},{6,5},{... | collective-permute-start | bytes 24584 | tf_op jit(solution)/shard_map/ppermute | solution.py:193
  2.0 5.3 %collective-permute-start.2 = (bf16[8,512]{1,0:T(8,128)(2,1)S(1)}, bf16[8,512]{1,0:T(8,128)(2,1)S(1)}, u32[]{:S(2)}, u32[]{:S(2)}) collective-permute-start(bf16[8,512]{1,0:T(8,128)(2,1)S(1)} %get-tuple-element.8), channel_id=1, source_target_pairs={{0,1},{1,0},{2,3},{3,2},{4,5},{5,4},{6,7},{7,6},{8,9},{9,8},{10,11... | collective-permute-start | bytes 24584 | tf_op jit(solution)/shard_map/ppermute | solution.py:192
  7.4 2.1 %convolution_convert_fusion.1 = bf16[512,1024]{0,1:T(8,128)(2,1)S(1)} fusion(bf16[1024,512]{1,0:T(8,128)(2,1)} %bitcast.19, bf16[512,512]{1,0:T(8,128)(2,1)} %constant.31.clone.refs_4_), kind=kOutput, calls=%fused_computation.1 | convolution fusion | flops 537395200 | bytes 2621440 | tf_op jit(solution)/shard_map/dot_general | solution.py:209
  9.5 0.0 copy-start
  9.5 0.0 copy-start.1
  9.5 0.0 copy-start.2
  9.5 0.0 copy-start.3
  9.5 0.0 copy-start.5
  9.5 0.0 copy-start.6
  9.5 0.0 copy-start.7
  9.5 0.0 collective-permute-done.1
  9.6 0.0 collective-permute-done.2
  9.6 0.1 collective-permute-start.3
  9.7 0.0 collective-permute-done
  9.7 0.0 copy-done.4
  9.7 0.7 %convolution_convert_fusion = bf16[512,1024]{0,1:T(8,128)(2,1)S(1)} fusion(bf16[1024,512]{1,0:T(8,128)(2,1)S(1)} %bitcast.20, bf16[512,512]{1,0:T(8,128)(2,1)S(1)} %copy-done.4), kind=kOutput, calls=%fused_computation | convolution fusion | flops 537395200 | bytes 2621440 | tf_op jit(solution)/shard_map/dot_general | solution.py:209
  10.4 0.4 %collective-permute-done.3.refs_3_ = bf16[16,512]{1,0:T(8,128)(2,1)S(1)} collective-permute-done((bf16[16,512]{1,0:T(8,128)(2,1)S(1)}, bf16[16,512]{1,0:T(8,128)(2,1)S(1)}, u32[]{:S(2)}, u32[]{:S(2)}) %collective-permute-start.3) | collective-permute-done | bytes 16416 | tf_op jit(solution)/shard_map/ppermute | solution.py:203
  10.8 0.0 copy-done
  10.8 0.0 copy-done.1
  10.9 0.0 copy-done.2
  10.9 0.0 copy-done.3
  10.9 19.2 %shard_map.91 = bf16[8,9,128,512]{3,2,1,0:T(8,128)(2,1)} custom-call(s32[1]{0:T(128)} %bitcast.block, s32[16]{0:T(128)S(1)} %copy-done.3, s32[16,9]{1,0:T(8,128)S(1)} %copy-done, s32[8,9]{1,0:T(8,128)S(1)} %copy-done.1, s32[8,9]{1,0:T(8,128)S(1)} %copy-done.2, bf16[8,128,512]{2,1,0:T(8,128)(2,1)S(1)} %bitcast.17, bf16[8,128,512]{2,1,0:T(8,128)(2,1)S(1)} %bitcast.18, ...), custom_call_target="tpu_custom_call" | custom-call | flops 9663676416 | bytes 9437184 | tf_op jit(solution)/shard_map/pallas_call | solution.py:169
  (7 shorter events, 0.0 us)
Async XLA Ops:
  0.0 9.7 %copy-start.4 = (bf16[512,512]{1,0:T(8,128)(2,1)S(1)}, bf16[512,512]{1,0:T(8,128)(2,1)}, u32[]{:S(2)}) copy-start(bf16[512,512]{1,0:T(8,128)(2,1)} %constant.31.clone.refs_4_) | copy-start | bytes 1572868
  0.0 9.7 %collective-permute-start = (bf16[8,128,512]{2,1,0:T(8,128)(2,1)}, bf16[8,128,512]{2,1,0:T(8,128)(2,1)S(1)}, u32[]{:S(2)}, u32[]{:S(2)}) collective-permute-start(bf16[8,128,512]{2,1,0:T(8,128)(2,1)} %param.9), channel_id=1, source_target_pairs={{16,0},{0,16},{17,1},{1,17},{18,2},{2,18},{19,3},{3,19},{20,4},{4,... | collective-permute-start | bytes 3145736 | tf_op jit(solution)/shard_map/ppermute | solution.py:203
  1.4 8.2 %collective-permute-start.1 = (bf16[8,512]{1,0:T(8,128)(2,1)S(1)}, bf16[8,512]{1,0:T(8,128)(2,1)S(1)}, u32[]{:S(2)}, u32[]{:S(2)}) collective-permute-start(bf16[8,512]{1,0:T(8,128)(2,1)S(1)} %get-tuple-element.7), channel_id=1, source_target_pairs={{1,2},{3,4},{5,6},{7,8},{9,10},{11,12},{13,14},{2,1},{4,3},{6,5},{... | collective-permute-start | bytes 24584 | tf_op jit(solution)/shard_map/ppermute | solution.py:193
  2.0 7.5 %collective-permute-start.2 = (bf16[8,512]{1,0:T(8,128)(2,1)S(1)}, bf16[8,512]{1,0:T(8,128)(2,1)S(1)}, u32[]{:S(2)}, u32[]{:S(2)}) collective-permute-start(bf16[8,512]{1,0:T(8,128)(2,1)S(1)} %get-tuple-element.8), channel_id=1, source_target_pairs={{0,1},{1,0},{2,3},{3,2},{4,5},{5,4},{6,7},{7,6},{8,9},{9,8},{10,11... | collective-permute-start | bytes 24584 | tf_op jit(solution)/shard_map/ppermute | solution.py:192
  9.5 1.4 %copy-start = (s32[16,9]{1,0:T(8,128)S(1)}, s32[16,9]{1,0:T(8,128)}, u32[]{:S(2)}) copy-start(s32[16,9]{1,0:T(8,128)} %partner.1) | copy-start | bytes 1732
  9.5 1.4 %copy-start.1 = (s32[8,9]{1,0:T(8,128)S(1)}, s32[8,9]{1,0:T(8,128)}, u32[]{:S(2)}) copy-start(s32[8,9]{1,0:T(8,128)} %low.1) | copy-start | bytes 868
  9.5 1.4 %copy-start.2 = (s32[8,9]{1,0:T(8,128)S(1)}, s32[8,9]{1,0:T(8,128)}, u32[]{:S(2)}) copy-start(s32[8,9]{1,0:T(8,128)} %high.1) | copy-start | bytes 868
  9.5 1.4 %copy-start.3 = (s32[16]{0:T(128)S(1)}, s32[16]{0:T(128)}, u32[]{:S(2)}) copy-start(s32[16]{0:T(128)} %count.1) | copy-start | bytes 196
  9.5 1.4 %copy-start.5 = (bf16[256,256]{1,0:T(8,128)(2,1)S(1)}, bf16[256,256]{1,0:T(8,128)(2,1)}, u32[]{:S(2)}) copy-start(bf16[256,256]{1,0:T(8,128)(2,1)} %constant.34.clone.refs_7_) | copy-start | bytes 393220
  9.5 1.4 %copy-start.6 = (bf16[256,256]{1,0:T(8,128)(2,1)S(1)}, bf16[256,256]{1,0:T(8,128)(2,1)}, u32[]{:S(2)}) copy-start(bf16[256,256]{1,0:T(8,128)(2,1)} %constant.33.clone.refs_6_) | copy-start | bytes 393220
  9.5 1.4 %copy-start.7 = (bf16[256,256]{1,0:T(8,128)(2,1)S(1)}, bf16[256,256]{1,0:T(8,128)(2,1)}, u32[]{:S(2)}) copy-start(bf16[256,256]{1,0:T(8,128)(2,1)} %constant.32.clone.refs_5_) | copy-start | bytes 393220
  9.6 1.2 %collective-permute-start.3 = (bf16[16,512]{1,0:T(8,128)(2,1)S(1)}, bf16[16,512]{1,0:T(8,128)(2,1)S(1)}, u32[]{:S(2)}, u32[]{:S(2)}) collective-permute-start(bf16[16,512]{1,0:T(8,128)(2,1)S(1)} %pad_maximum_fusion.refs_2_), channel_id=1, source_target_pairs={{16,0},{0,16},{17,1},{1,17},{18,2},{2,18},{19,3},{3,19},{20,4},{4,... | collective-permute-start | bytes 49160 | tf_op jit(solution)/shard_map/ppermute | solution.py:203
